TPU v7x, 32 devices: a whole 2x2x4 slice. The times are simulated.
32 devices in a mesh: seq: 16 (over z, y, x), tp: 2 (over core).
Axes of the slice: x: 2, y: 2, z: 4, core: 2. Of those that a mesh axis runs over, the one named last changes fastest.
Arguments:
- x_proj: bfloat16 [8192, 8192], P('seq', 'tp'), may hold values from -27 to 27
- bc_proj: bfloat16 [8192, 2, 1024], P('seq', None, 'tp'), may hold values from -6 to 6
- z_proj: bfloat16 [8192, 8192], P('seq', 'tp'), may hold values from -6 to 6
- dt_raw: float32 [8192, 128], P('seq', 'tp'), may hold values from -2.5 to 63
- conv_x: bfloat16 [4, 8192], P(None, 'tp'), may hold values from -3 to 3
- conv_bc: bfloat16 [4, 2, 1024], P(None, None, 'tp'), may hold values from -3 to 3
- bias_x: float32 [8192], P('tp'), may hold values from -0.5 to 0.5
- bias_bc: float32 [2, 1024], P(None, 'tp'), may hold values from -0.5 to 0.5
- dt_bias: float32 [128], P('tp'), may hold values from -4.5 to -3
- a_log: float32 [128], P('tp'), may hold values from -5.5 to 0.5
- d_skip: float32 [128], P('tp'), may hold values from 0.15 to 5
- norm_gain: float32 [8192], P('tp'), may hold values from 0.1 to 1.9
- seg_ids: int32 [8192], P('seq'), may hold values from 0 to 15, never falling along the last dimension, each value on 1 to 2048 neighbouring positions
Outputs:
- normed: bfloat16 [8192, 8192], P('seq', 'tp')
Inputs may be any that keep to these rules, and one draw needn't show every extreme that they name: `seg_ids`: each prompt's tokens are contiguous; ids start at 0 and never fall, each id from 0 to 15 has one token or more, at most 2048 tokens, and one prompt has exactly 2048.
All inputs are finite; a program needn't handle non-finite values.
Results may differ from a plain program's by a relative error of at most 0.0036.
Values may be sent and summed in bfloat16 or wider, within the bound.
A program may use at most 128 MiB of HBM per device.

v0:
```python
import jax
import jax.numpy as jnp
from jax import lax
from jax.sharding import PartitionSpec as P

STATE = 128
STRETCH = 256


def from_behind(block, axis, distance):
    devices = range(lax.axis_size(axis))
    route = [(i - distance, i) for i in devices if i - distance in devices]
    return lax.ppermute(block, axis, route)


def carried_in(value, axis, join, neutral):
    count, mine = (lax.axis_size(axis), lax.axis_index(axis))
    pieces = jax.tree.map(lambda part: lax.all_gather(part, axis), value)
    running = jax.tree.map(
        lambda part, zero: jnp.full_like(part, 0) + jnp.asarray(zero, part.dtype), value, neutral
    )

    def step(position, running):
        longer = join(running, jax.tree.map(lambda part: part[position], pieces))
        return jax.tree.map(lambda new, old: jnp.where(position < mine, new, old), longer, running)

    return lax.fori_loop(0, count - 1, step, running)


def causal_conv(window, window_ids, weight, bias, rows):
    taps = weight.shape[0]
    own_ids = window_ids[taps - 1 :]
    extra = (1,) * (window.ndim - 1)
    result = jnp.broadcast_to(bias, (rows,) + bias.shape)
    for offset in range(taps):
        piece = window[offset : offset + rows].astype(jnp.float32)
        same = (window_ids[offset : offset + rows] == own_ids).reshape((rows,) + extra)
        result = result + jnp.where(same, piece * weight[offset].astype(jnp.float32), 0.0)
    return jax.nn.silu(result).astype(jnp.bfloat16)


def on_device(
    x_proj,
    bc_proj,
    z_proj,
    dt_raw,
    conv_x,
    conv_bc,
    bias_x,
    bias_bc,
    dt_bias,
    a_log,
    d_skip,
    norm_gain,
    seg_ids,
):
    tok_rows, inner_local = x_proj.shape
    heads_local = dt_raw.shape[1]
    state_size = STATE
    groups_local = bc_proj.shape[2] // state_size
    heads_group = heads_local // groups_local
    head_size = inner_local // heads_local
    block = STRETCH
    blocks = tok_rows // block
    margin = conv_x.shape[0] - 1
    tails = (
        x_proj[tok_rows - margin :],
        bc_proj[tok_rows - margin :],
        seg_ids[tok_rows - margin :].astype(jnp.bfloat16),
    )
    rim_x, rim_bc, rim_ids = from_behind((tails[0], tails[1], tails[2]), "seq", 1)
    own_ids = seg_ids.astype(jnp.float32)
    window_ids = jnp.concatenate([rim_ids.astype(jnp.float32), own_ids])
    x_conv = causal_conv(jnp.concatenate([rim_x, x_proj]), window_ids, conv_x, bias_x, tok_rows)
    bc_conv = causal_conv(
        jnp.concatenate([rim_bc, bc_proj]), window_ids, conv_bc, bias_bc, tok_rows
    )
    step_size = jax.nn.softplus(dt_raw + dt_bias)
    log_decay = step_size * -jnp.exp(a_log)
    cumul = jnp.cumsum(log_decay.reshape(blocks, block, heads_local), axis=1)
    cum_heads = cumul.reshape(blocks, block, groups_local, heads_group).transpose(0, 2, 3, 1)
    step_heads = step_size.reshape(blocks, block, groups_local, heads_group).transpose(0, 2, 3, 1)
    block_ids = own_ids.reshape(blocks, block)
    before_ids = window_ids[margin - 1 : margin - 1 + tok_rows : block]
    b_in = bc_conv[:, 0].reshape(blocks, block, groups_local, state_size)
    c_out = bc_conv[:, 1].reshape(blocks, block, groups_local, state_size)
    lower = jnp.tril(jnp.ones((block, block), dtype=bool))
    same = (block_ids[:, :, None] == block_ids[:, None, :]) & lower
    scores = jnp.einsum("cqgn,csgn->cgqs", c_out, b_in, preferred_element_type=jnp.float32)
    same_heads = same[:, None, None]
    spread = cum_heads[..., :, None] - cum_heads[..., None, :]
    decay = jnp.where(same_heads, jnp.exp(jnp.where(same_heads, spread, 0.0)), 0.0)
    mixing = (scores[:, :, None] * decay * step_heads[..., None, :]).astype(jnp.bfloat16)
    x_heads = x_conv.reshape(blocks, block, groups_local, heads_group, head_size)
    y_intra = jnp.einsum("cghqs,csghp->cqghp", mixing, x_heads, preferred_element_type=jnp.float32)
    tail_same = (block_ids == block_ids[:, -1:]).astype(jnp.float32)[:, None, None, :]
    weights = jnp.exp(cum_heads[..., -1:] - cum_heads) * step_heads * tail_same
    b_weighted = (
        b_in.transpose(0, 2, 1, 3)[:, :, None].astype(jnp.float32) * weights[..., None]
    ).astype(jnp.bfloat16)
    increment = jnp.einsum(
        "cghsn,csghp->cghpn", b_weighted, x_heads, preferred_element_type=jnp.float32
    )
    carry_gain = (
        jnp.exp(cum_heads[..., -1])
        * (block_ids[:, -1] == before_ids).astype(jnp.float32)[:, None, None]
    )
    link = (
        jnp.exp(cum_heads)
        * (block_ids == before_ids[:, None]).astype(jnp.float32)[:, None, None, :]
    )
    c_float = c_out.astype(jnp.float32)

    def recur(start_state):
        stacked = []
        current = start_state
        for index in range(blocks):
            stacked.append(current)
            current = carry_gain[index][..., None, None] * current + increment[index]
        return (jnp.stack(stacked), current)

    empty = jnp.zeros((groups_local, heads_group, head_size, state_size), jnp.float32)
    zero_states, summary = recur(empty)
    device_gain = carry_gain[0]
    index = 1
    device_gain = device_gain * carry_gain[index]

    def combine(earlier, later):
        return (earlier[0] * later[0], later[0][..., None, None] * earlier[1] + later[1])

    identity = (jnp.ones_like(device_gain), empty)
    _, entering = carried_in((device_gain, summary), "seq", combine, identity)
    states, _ = recur(entering)
    product = jnp.einsum("cqgn,cghpn->cqghp", c_float, states, precision=lax.Precision.HIGHEST)
    y_inter = product * link.transpose(0, 3, 1, 2)[..., None]
    skip = d_skip.reshape(groups_local, heads_group)[..., None]
    mixed = y_intra + y_inter + skip * x_heads.astype(jnp.float32)
    gated = mixed.reshape(tok_rows, inner_local) * jax.nn.silu(z_proj.astype(jnp.float32))
    squares = lax.psum(jnp.sum(gated * gated, axis=-1), "tp")
    scale = lax.rsqrt(squares / (inner_local * lax.axis_size("tp")) + 1e-05)
    return (gated * scale[:, None] * norm_gain).astype(jnp.bfloat16)


def solution(mesh):
    in_specs = (
        P("seq", "tp"),
        P("seq", None, "tp"),
        P("seq", "tp"),
        P("seq", "tp"),
        P(None, "tp"),
        P(None, None, "tp"),
        P("tp"),
        P(None, "tp"),
        P("tp"),
        P("tp"),
        P("tp"),
        P("tp"),
        P("seq"),
    )
    out_specs = P("seq", "tp")
    return jax.shard_map(
        on_device, mesh=mesh, in_specs=in_specs, out_specs=out_specs, check_vma=False
    )
```

profile of v0, /device:TPU:0, one launch (start us, length us, event | category | flops | bytes accessed | tf_op | source)
XLA Modules:
  0.0 530.7 jit_solution(2024596497389895188)
XLA Ops:
  6.5 0.8 fusion.33
  7.4 4.8 collective-permute-start
  12.2 0.7 slice.115
  12.9 3.4 collective-permute-start.2
  16.3 0.9 slice.105
  17.3 3.5 collective-permute-start.1
  20.8 6.4 %copy.55 = bf16[512,4096]{0,1:T(8,128)(2,1)} copy(bf16[512,4096]{1,0:T(8,128)(2,1)} %param.15) | data formatting | bytes 8388608 | tf_op args[0]
  27.7 1.2 reduce-window.6
  30.1 0.8 constant_dynamic-update-slice_fusion
  30.9 7.9 %fusion.26 = bf16[512,2,512]{2,1,0:T(2,128)(2,1)S(1)} fusion(bf16[512,2,512]{2,1,0:T(2,128)(2,1)S(1)} %copy-done.3, pred[512]{0:T(512)(128)(4,1)S(1)} %get-tuple-element.148, pred[512]{0:T(512)(128)(4,1)S(1)} %get-tuple-element.141, pred[512]{0:T(512)(128)(4,1)S(1)} %get-tuple-element.142, pred[512]{0:T(512)(128)(4,1)S(1)} %get-tuple-element.140, ...), kind=kLoop, calls=%fused_computation.44 | loop fusion | flops 11010048 | bytes 5265408 | tf_op jit(solution)/shard_map/convert_element_type | solution.py:39
  38.9 6.5 %slice_reduce_fusion.1 = (bf16[512,512]{1,0:T(8,128)(2,1)}, bf16[512,512]{1,0:T(8,128)(2,1)S(1)}) fusion(bf16[512,2,512]{2,1,0:T(2,128)(2,1)S(1)} %fusion.26), kind=kLoop, calls=%fused_computation.46 | loop fusion | bytes 2097152 | tf_op jit(solution)/shard_map/slice | solution.py:86
  45.7 0.5 copy.54
  46.2 16.4 %multiply_convert_fusion.5 = bf16[512,4096]{0,1:T(8,128)(2,1)} fusion(bf16[512,4096]{0,1:T(8,128)(2,1)} %copy.55, bf16[3,4096]{0,1:T(8,128)(2,1)S(1)} %copy.54, f32[4096]{0:T(1024)S(1)} %bitcast.98, f32[4096]{0:T(1024)S(1)} %bitcast.99, f32[4096]{0:T(1024)S(1)} %bitcast.97, f32[4096]{0:T(1024)S(1)} %bitcast.96, f32[4096]{0:T(1024)S(1)} %copy-done.9, ...), kind=kLoop, calls=%fused_computation.26 | loop fusion | flops 62914560 | bytes 8497152 | tf_op jit(solution)/shard_map/convert_element_type | solution.py:39
  62.7 6.9 %reshape.105 = bf16[2,256,4,16,64]{1,0,4,3,2:T(2,128)(2,1)} reshape(bf16[512,4096]{0,1:T(8,128)(2,1)} %multiply_convert_fusion.5) | data formatting | bytes 8388608 | tf_op jit(solution)/shard_map/reshape | solution.py:94
  69.5 8.5 %fusion.12 = f32[2,4,16,64,128]{4,3,2,1,0:T(8,128)S(1)} fusion(f32[2,4,16,256]{3,2,1,0:T(8,128)S(1)} %multiply_multiply_fusion, f32[2,4,256,128]{3,2,1,0:T(8,128)S(1)} %copy.64, bf16[2,256,4,16,64]{1,0,4,3,2:T(2,128)(2,1)} %reshape.105), kind=kOutput, calls=%fused_computation.18 | convolution fusion | flops 545259520 | bytes 9568256 | tf_op jit(solution)/shard_map/cghsn,csghp->cghpn/dot_general | solution.py:101
  78.0 2.0 copy-done.2
  80.1 1.6 slice_add_fusion
  81.9 6.5 %copy.69 = bf16[512,4096]{0,1:T(8,128)(2,1)} copy(bf16[512,4096]{1,0:T(8,128)(2,1)} %param.17) | data formatting | bytes 8388608 | tf_op args[2]
  88.5 41.0 %all_gather.8 = f32[16,4,16]{2,1,0:T(4,128)} all-gather(f32[1,4,16]{2,1,0:T(4,128)S(1)} %get-tuple-element.145), channel_id=1, replica_groups=mesh['seq'=16,'tp'=2] {'seq'}, dimensions={0}, use_global_device_ids=true | all-gather | bytes 4352 | tf_op jit(solution)/shard_map/all_gather | solution.py:18
  129.5 0.7 copy_bitcast_fusion.2
  130.2 1.2 reshape_squeeze.6
  131.3 1.8 fusion.28
  133.1 299.9 %all-gather.2.cloned.1.call-done = f32[16,4,16,64,128]{4,3,2,1,0:T(8,128)} async-done(((f32[1,4,16,64,128]{4,3,2,1,0:T(8,128)}), f32[16,4,16,64,128]{4,3,2,1,0:T(8,128)}) %all-gather.2.cloned.1.call-update) | async-done | bytes 33554448 | tf_op jit(solution)/shard_map/all_gather | solution.py:18
  433.1 41.6 %while.14 = (s32[]{:T(128)}, f32[4,16,64,128]{3,2,1,0:T(8,128)S(1)}, s32[]{:T(128)}, f32[16,4,16]{2,1,0:T(4,128)}, f32[16,4,16,64,128]{4,3,2,1,0:T(8,128)}, /*index=5*/s32[]{:T(128)}, s32[]{:T(128)}) while((s32[]{:T(128)}, f32[4,16,64,128]{3,2,1,0:T(8,128)S(1)}, s32[]{:T(128)}, f32[16,4,16]{2,1,0:T(4,128)}, ...), condition=%wide.region_3.4_spmd.clone, body=%wide.region_2.3_spmd.clone.sunk | while | flops 2097156 | bytes 6292329 | solution.py:27
  433.1 0.7 dynamic-slice_bitcast_fusion.2
  433.8 2.1 fusion.35
  435.8 0.7 dynamic-slice_bitcast_fusion.2
  436.5 2.1 fusion.35
  438.6 0.7 dynamic-slice_bitcast_fusion.2
  439.3 2.1 fusion.35
  441.4 0.7 dynamic-slice_bitcast_fusion.2
  442.1 2.1 fusion.35
  444.2 0.7 dynamic-slice_bitcast_fusion.2
  444.8 2.1 fusion.35
  446.9 0.7 dynamic-slice_bitcast_fusion.2
  447.6 2.1 fusion.35
  449.7 0.7 dynamic-slice_bitcast_fusion.2
  450.4 2.1 fusion.35
  452.5 0.7 dynamic-slice_bitcast_fusion.2
  453.1 2.1 fusion.35
  455.2 0.7 dynamic-slice_bitcast_fusion.2
  455.9 2.1 fusion.35
  458.0 0.7 dynamic-slice_bitcast_fusion.2
  458.7 2.1 fusion.35
  460.8 0.7 dynamic-slice_bitcast_fusion.2
  461.5 2.1 fusion.35
  463.6 0.7 dynamic-slice_bitcast_fusion.2
  464.2 2.1 fusion.35
  466.3 0.7 dynamic-slice_bitcast_fusion.2
  467.0 2.1 fusion.35
  469.1 0.7 dynamic-slice_bitcast_fusion.2
  469.8 2.1 fusion.35
  471.9 0.7 dynamic-slice_bitcast_fusion.2
  472.6 2.1 fusion.35
  474.6 1.9 fusion.25
  476.5 3.6 fusion.19
  480.2 12.4 %fusion.14 = f32[2,256,4,16,64]{1,4,3,2,0:T(8,128)S(1)} fusion(f32[2,4,16,64,256]{4,3,2,1,0:T(8,128)S(1)} %fusion.19, f32[4,16]{1,0:T(4,128)S(1)} %mul.339, f32[2,256,4,16]{1,3,2,0:T(8,128)S(1)} %copy-done.8, f32[2,4,16,256]{3,2,1,0:T(8,128)S(1)} %get-tuple-element.151, f32[2,4,16,256]{3,2,1,0:T(8,128)S(1)} %bitcast.94, ...), kind=kOutput, calls=%fused_computation.21 | convolution fusion | flops 1134559232 | bytes 23593216 | tf_op jit(solution)/shard_map/cghqs,csghp->cqghp/dot_general | solution.py:95
  492.6 7.9 %copy.68 = f32[2,256,4,16,64]{1,0,4,3,2:T(2,128)S(1)} copy(f32[2,256,4,16,64]{1,4,3,2,0:T(8,128)S(1)} %fusion.14) | data formatting | bytes 16777216 | tf_op jit(solution)/shard_map/add | solution.py:137
  500.5 1.0 copy.77
  501.5 3.2 copy-done
  504.8 2.9 multiply_reduce_fusion
  507.6 2.5 psum.7
  510.1 7.4 %multiply_convert_fusion.4 = bf16[512,4096]{0,1:T(8,128)(2,1)} fusion(f32[4096]{0:T(1024)S(1)} %copy-done.10, f32[512]{0:T(512)S(1)} %add_rsqrt_fusion, f32[512,4096]{0,1:T(8,128)} %bitcast.89, bf16[512,4096]{0,1:T(8,128)(2,1)} %copy.69), kind=kLoop, calls=%fused_computation.22 | loop fusion | flops 18874368 | bytes 16795648 | tf_op jit(solution)/shard_map/convert_element_type | solution.py:141
  517.5 6.3 %copy.70 = bf16[512,4096]{1,0:T(8,128)(2,1)} copy(bf16[512,4096]{0,1:T(8,128)(2,1)} %multiply_convert_fusion.4) | data formatting | bytes 8388608 | tf_op jit(solution)/shard_map/convert_element_type | solution.py:141
  (70 shorter events, 2.3 us)
Async XLA Ops:
  6.5 426.5 %all-gather.2.cloned.1.call-start = ((), (), s32[]{:S(2)}) async-start(), calls=%async_computation | async-start | bytes 35651584 | tf_op jit(solution)/shard_map/all_gather | solution.py:18
  7.4 22.2 %collective-permute-start = (bf16[3]{0:T(256)(128)(2,1)S(1)}, bf16[3]{0:T(256)(128)(2,1)S(1)}, u32[]{:S(2)}, u32[]{:S(2)}) collective-permute-start(bf16[3]{0:T(256)(128)(2,1)S(1)} %slice.103), channel_id=1, source_target_pairs={{0,2},{2,4},{4,6},{6,8},{8,10},{10,12},{12,14},{14,16},{16,18},{18... | collective-permute-start | bytes 26 | tf_op jit(solution)/shard_map/ppermute | solution.py:13
  12.9 17.2 %collective-permute-start.2 = (bf16[3,2,512]{2,1,0:T(2,128)(2,1)S(1)}, bf16[3,2,512]{2,1,0:T(2,128)(2,1)S(1)}, u32[]{:S(2)}, u32[]{:S(2)}) collective-permute-start(bf16[3,2,512]{2,1,0:T(2,128)(2,1)S(1)} %slice.115), channel_id=1, source_target_pairs={{0,2},{2,4},{4,6},{6,8},{8,10},{10,12},{12,14},{14,16},{16,18},{18... | collective-permute-start | bytes 18440 | tf_op jit(solution)/shard_map/ppermute | solution.py:13
  17.2 10.0 %copy-start.11 = (bf16[4,2,512]{2,1,0:T(2,128)(2,1)S(1)}, bf16[4,2,512]{2,1,0:T(2,128)(2,1)}, u32[]{:S(2)}) copy-start(bf16[4,2,512]{2,1,0:T(2,128)(2,1)} %param.20) | copy-start | bytes 24580
  17.2 10.0 %copy-start.7 = (bf16[4,4096]{1,0:T(4,128)(2,1)S(1)}, bf16[4,4096]{1,0:T(4,128)(2,1)}, u32[]{:S(2)}) copy-start(bf16[4,4096]{1,0:T(4,128)(2,1)} %param.19) | copy-start | bytes 98308
  17.2 10.3 %copy-start.16 = (f32[64]{0:T(128)S(1)}, f32[64]{0:T(128)}, u32[]{:S(2)}) copy-start(f32[64]{0:T(128)} %param.24) | copy-start | bytes 772
  17.2 10.3 %copy-start.6 = (f32[512,64]{0,1:T(8,128)S(1)}, f32[512,64]{0,1:T(8,128)}, u32[]{:S(2)}) copy-start(f32[512,64]{0,1:T(8,128)} %param.18) | copy-start | bytes 393220
  17.2 10.3 %copy-start.14 = (f32[64]{0:T(128)S(1)}, f32[64]{0:T(128)}, u32[]{:S(2)}) copy-start(f32[64]{0:T(128)} %param.23) | copy-start | bytes 772
  17.2 12.4 %copy-start.12 = (s32[512]{0:T(512)S(1)}, s32[512]{0:T(512)}, u32[]{:S(2)}) copy-start(s32[512]{0:T(512)} %param.27) | copy-start | bytes 6148
  17.2 12.9 %copy-start.3 = (bf16[512,2,512]{2,1,0:T(2,128)(2,1)S(1)}, bf16[512,2,512]{2,1,0:T(2,128)(2,1)}, u32[]{:S(2)}) copy-start(bf16[512,2,512]{2,1,0:T(2,128)(2,1)} %param.16) | copy-start | bytes 3145732
  17.3 28.4 %collective-permute-start.1 = (bf16[3,4096]{1,0:T(4,128)(2,1)S(1)}, bf16[3,4096]{1,0:T(4,128)(2,1)S(1)}, u32[]{:S(2)}, u32[]{:S(2)}) collective-permute-start(bf16[3,4096]{1,0:T(4,128)(2,1)S(1)} %slice.105), channel_id=1, source_target_pairs={{0,2},{2,4},{4,6},{6,8},{8,10},{10,12},{12,14},{14,16},{16,18},{18... | collective-permute-start | bytes 73736 | tf_op jit(solution)/shard_map/ppermute | solution.py:13
  27.2 3.7 copy-start.13
  38.9 7.3 %copy-start.9 = (f32[4096]{0:T(1024)S(1)}, f32[4096]{0:T(1024)}, u32[]{:S(2)}) copy-start(f32[4096]{0:T(1024)} %param.21) | copy-start | bytes 49156
  78.0 2.0 copy-start.2
  80.1 1.7 copy-start.15
  476.5 3.7 copy-start.4
  476.5 3.7 copy-start.5
  476.5 3.7 copy-start.8
  500.5 4.3 copy-start.1
  501.5 3.2 copy-start
  504.8 5.4 %copy-start.10 = (f32[4096]{0:T(1024)S(1)}, f32[4096]{0:T(1024)}, u32[]{:S(2)}) copy-start(f32[4096]{0:T(1024)} %param.26) | copy-start | bytes 49156
Sparse Core Ops, SparseCore 0:
  81.9 351.1 all-gather.1
where the time goes:
time: 533 us; the launch traced here: 531 us
  waiting for transfers between devices  300 us (56%)
  other arithmetic  73 us (14%)
  local copies, waits for them, and re-layouts  62.1 us (12%)
  blocking collectives  43.4 us (8%)
  matrix products  26.3 us (5%)
  between operations  13.8 us (3%)
  starting transfers between devices  11.8 us (2%)
    all_gather x1, waiting for transfers between devices, carried_in(): pieces = jax.tree.map(lambda part: lax.all_gather(part, axis), value)  300 us
    all_gather x1, blocking collectives, carried_in(): pieces = jax.tree.map(lambda part: lax.all_gather(part, axis), value)  41 us
    select_n x15, other arithmetic, step(): jnp.where(position < mine, new, old)  31.1 us
    convert_element_type x2, other arithmetic, causal_conv(): return jax.nn.silu(result).astype(jnp.bfloat16)  24.4 us
    unnamed x38, local copies, waits for them, and re-layouts  19.3 us
    dot_general x1, matrix products, on_device(): jnp.einsum('cghqs,csghp->cqghp', mixing, x_heads, preferred_element_type=...  12.4 us
    ppermute x3, starting transfers between devices, from_behind(): return lax.ppermute(block, axis, route)  11.8 us
  transfers between devices with their start and end apart: 4, of which 1 were waited for; matrix products, arithmetic and copies ran while one was open for 7% of the time, Pallas kernels for 0%

commit v1 on v0

v1 whole, which is shorter than its diff:
```python
import jax
import jax.numpy as jnp
from jax import lax
from jax.experimental import pallas as pl
from jax.experimental.pallas import tpu as pltpu
from jax.sharding import PartitionSpec as P

STATE = 128
STRETCH = 256
RIM = 8
LOG2E = 1.4426950408889634
F32 = jnp.float32
BF16 = jnp.bfloat16
VMEM = 52 * 1024 * 1024


def silu(v):
    half = 0.5 * v
    return half * jnp.tanh(half) + half


def conv_tile(window, weight, bias, masks, start, rows, lanes):
    acc = jnp.broadcast_to(bias, (rows, lanes.stop - lanes.start))
    for tap in range(4):
        piece = window[pl.ds(RIM - 3 + tap + start, rows), lanes]
        term = piece * weight[tap : tap + 1]
        if tap < 3:
            term = term * masks[tap, pl.ds(start, rows), :]
        acc = acc + term
    return silu(acc).astype(BF16)


def local_kernel(
    x_ref, rim_ref, b_ref, c_ref, rimb_ref, rimc_ref, wx_ref, wb_ref, wc_ref,
    bx_ref, bb_ref, bc_ref, masks, tail_ref, gain_ref, row_gain_ref, expand_ref,
    xo_ref, bo_ref, co_ref, inc_ref, sum_ref, window, window_b, window_c, weighted,
):
    rows, width = x_ref.shape
    blocks = rows // STRETCH
    window[0:RIM] = rim_ref[...].astype(F32)
    window_b[0:RIM] = rimb_ref[...].astype(F32)
    window_c[0:RIM] = rimc_ref[...].astype(F32)
    window_b[RIM:] = b_ref[...].astype(F32)
    window_c[RIM:] = c_ref[...].astype(F32)
    one = slice(0, STATE)
    for block in range(blocks):
        at = slice(block * STRETCH, (block + 1) * STRETCH)
        bo_ref[at] = conv_tile(
            window_b, wb_ref[...].astype(F32), bb_ref[...], masks, at.start, STRETCH, one
        )
        co_ref[at] = conv_tile(
            window_c, wc_ref[...].astype(F32), bc_ref[...], masks, at.start, STRETCH, one
        )
    for tile in range(width // 128):
        lanes = slice(tile * 128, (tile + 1) * 128)
        window[RIM:, lanes] = x_ref[:, lanes].astype(F32)
        weight = wx_ref[:, lanes].astype(F32)
        for block in range(blocks):
            at = slice(block * STRETCH, (block + 1) * STRETCH)
            value = conv_tile(window, weight, bx_ref[:, lanes], masks, at.start, STRETCH, lanes)
            xo_ref[at, lanes] = value
            spread = jnp.dot(
                tail_ref[0, at, :], expand_ref[:, lanes], preferred_element_type=F32
            )
            weighted[at, lanes] = (value.astype(F32) * spread).astype(BF16)
    parts = []
    for block in range(blocks):
        at = slice(block * STRETCH, (block + 1) * STRETCH)
        parts.append(
            lax.dot_general(
                bo_ref[at], weighted[at], (((0,), (0,)), ((), ())), preferred_element_type=F32
            )
        )
    inc_ref[0] = parts[0]
    sum_ref[0, 0:STATE] = (row_gain_ref[1:2] * parts[0] + parts[1]).astype(BF16)
    sum_ref[0, STATE:] = gain_ref[0]


def intra_kernel(
    x_ref, b_ref, c_ref, col_ref, row_ref, ids_ref, idr_ref, skip_ref, y_ref
):
    rows, width = x_ref.shape
    blocks = rows // STRETCH
    half = STRETCH // 2
    lane = lax.broadcasted_iota(jnp.int32, (STRETCH, 128), 1)
    first = lane < 64
    t_at = lax.broadcasted_iota(jnp.int32, (STRETCH, STRETCH), 0)
    s_at = lax.broadcasted_iota(jnp.int32, (STRETCH, STRETCH), 1)
    lower = s_at <= t_at
    for block in range(blocks):
        at = slice(block * STRETCH, (block + 1) * STRETCH)
        scores = lax.dot_general(
            c_ref[at], b_ref[at], (((1,), (1,)), ((), ())), preferred_element_type=F32
        )
        same = (ids_ref[at] == idr_ref[block : block + 1]) & lower
        scores = jnp.where(same, scores, 0.0)
        top, left, right = scores[:half, :half], scores[half:, :half], scores[half:, half:]
        for pair in range(width // 128):
            lanes = slice(pair * 128, (pair + 1) * 128)
            value = x_ref[at, lanes]
            upper_sum = lower_sum = None
            for which in range(2):
                head = 2 * pair + which
                keep = first if which == 0 else jnp.logical_not(first)
                mine = jnp.where(keep, value.astype(F32), 0.0).astype(BF16)
                col = col_ref[0, at, head : head + 1]
                row = row_ref[0, block, head : head + 1, :]
                m_top = top * jnp.exp2(jnp.minimum(col[:half] - row[:, :half], 80.0))
                m_left = left * jnp.exp2(col[half:] - row[:, :half])
                m_right = right * jnp.exp2(jnp.minimum(col[half:] - row[:, half:], 80.0))
                m_low = jnp.concatenate([m_left.astype(BF16), m_right.astype(BF16)], axis=1)
                up = jnp.dot(m_top.astype(BF16), mine[:half], preferred_element_type=F32)
                low = jnp.dot(m_low, mine, preferred_element_type=F32)
                upper_sum = up if which == 0 else upper_sum + up
                lower_sum = low if which == 0 else lower_sum + low
            skip = skip_ref[:, lanes]
            wide = value.astype(F32)
            y_ref[at.start : at.start + half, lanes] = upper_sum + skip * wide[:half]
            y_ref[at.start + half : at.stop, lanes] = lower_sum + skip * wide[half:]


def gate_kernel(
    y_ref, z_ref, c_ref, link_ref, expand_ref, enter_ref, inc_ref, row_gain_ref, out_ref, sq_ref
):
    rows, width = y_ref.shape
    blocks = rows // STRETCH

    @pl.when(pl.program_id(0) == 0)
    def _():
        sq_ref[...] = jnp.zeros_like(sq_ref)

    for tile in range(width // 256):
        lanes = slice(tile * 256, (tile + 1) * 256)
        state = enter_ref[0, :, lanes]
        for block in range(blocks):
            at = slice(block * STRETCH, (block + 1) * STRETCH)
            if block == 1:
                state = (
                    row_gain_ref[0:1, lanes] * state.astype(F32) + inc_ref[0, :, lanes]
                ).astype(BF16)
            inter = jnp.dot(c_ref[at], state, preferred_element_type=F32)
            link = jnp.dot(link_ref[0, at], expand_ref[:, lanes], preferred_element_type=F32)
            gate = silu(z_ref[at, lanes].astype(F32))
            gated = (y_ref[at, lanes] + inter * link) * gate
            out_ref[at, lanes] = gated
            square = gated * gated
            sq_ref[at] += square[:, :128] + square[:, 128:]


def split_two(value):
    high = value.astype(BF16)
    return jnp.concatenate([high, (value - high.astype(F32)).astype(BF16)], axis=-1)


def exchange(sums, groups):
    axis = "seq"
    count = lax.axis_size(axis)
    plane = count // 4
    mine = lax.axis_index(axis)
    place = mine % plane
    _, depth, width = sums.shape
    cut = groups * width // plane
    split = plane // groups
    chunks = sums.reshape(groups, depth, split, cut).transpose(0, 2, 1, 3)
    chunks = chunks.reshape(plane, depth, cut)

    def pick(array, index):
        return lax.dynamic_index_in_dim(array, index, 0, keepdims=False)

    def swap(array):
        got = [pick(array, place)]
        for k in range(1, plane):
            got.append(
                lax.ppermute(pick(array, place ^ k), axis, [(i, i ^ k) for i in range(count)])
            )
        return jnp.stack(got)

    came = swap(chunks)
    run = jnp.zeros((STATE, cut), F32)
    through = jnp.ones((1, cut), F32)
    entering, gains = [], []
    for source in range(plane):
        part = pick(came, place ^ source)
        gain = part[STATE : STATE + 1].astype(F32) + part[STATE + 1 : STATE + 2].astype(F32)
        entering.append(run)
        gains.append(through)
        run = gain * run + part[:STATE].astype(F32)
        through = through * gain
    before = lax.ppermute(
        run.astype(BF16), axis, [(i, i + plane) for i in range(count - plane)]
    ).astype(F32)
    ready = jnp.stack([(e + g * before).astype(BF16) for e, g in zip(entering, gains)])
    back = swap(ready)
    final = jnp.stack([pick(back, place ^ owner) for owner in range(plane)])
    final = final.reshape(groups, split, STATE, cut).transpose(0, 2, 1, 3)
    return final.reshape(groups, STATE, width)


def on_device(
    x_proj, bc_proj, z_proj, dt_raw, conv_x, conv_bc, bias_x, bias_bc, dt_bias, a_log,
    d_skip, norm_gain, seg_ids,
):
    rows, inner = x_proj.shape
    heads = dt_raw.shape[1]
    groups = bc_proj.shape[2] // STATE
    per = heads // groups
    size = inner // heads
    width = inner // groups
    blocks = rows // STRETCH
    seq = lax.axis_size("seq")
    bc_flat = bc_proj.reshape(rows, 2 * groups * STATE)
    wbc = conv_bc.reshape(4, 2 * groups * STATE)
    bbc = bias_bc.reshape(1, 2 * groups * STATE)
    route = [(i, i + 1) for i in range(seq - 1)]
    rim_x = lax.ppermute(x_proj[rows - RIM :], "seq", route)
    rim_bc = lax.ppermute(bc_flat[rows - RIM :], "seq", route)
    rim_ids = lax.ppermute(seg_ids[rows - RIM :], "seq", route)
    window_ids = jnp.concatenate([rim_ids, seg_ids])
    masks = jnp.stack(
        [(window_ids[RIM - 3 + k : RIM - 3 + k + rows] == seg_ids).astype(F32) for k in range(3)]
    )
    masks = jnp.broadcast_to(masks[:, :, None], (3, rows, 128))

    step = jax.nn.softplus(dt_raw + dt_bias)
    rate = -jnp.exp(a_log) * LOG2E
    tri = jnp.tril(jnp.ones((STRETCH, STRETCH), F32))
    logs = (step * rate).reshape(blocks, STRETCH, heads)
    cum = jnp.einsum("ts,csh->cth", tri, logs, precision=lax.Precision.HIGHEST)
    last = cum[:, -1:]
    ids = seg_ids.reshape(blocks, STRETCH)
    before = window_ids[RIM - 1 : RIM - 1 + rows : STRETCH]
    steps = step.reshape(blocks, STRETCH, heads)
    tail = jnp.exp2(last - cum) * steps * (ids == ids[:, -1:]).astype(F32)[..., None]
    link = jnp.exp2(cum) * (ids == before[:, None]).astype(F32)[..., None]
    gain = jnp.exp2(last[:, 0]) * (ids[:, -1] == before).astype(F32)[:, None]

    def by_group(value):
        return value.reshape(rows, groups, per).transpose(1, 0, 2)

    tail_two = split_two(by_group(tail))
    link_two = split_two(by_group(link))
    col = by_group(cum)
    shifted = cum - jnp.log2(steps)
    row = shifted.reshape(blocks, STRETCH, groups, per).transpose(2, 0, 3, 1)
    row_gain = jnp.repeat(gain, size, axis=1)
    whole = row_gain[0] * row_gain[1]
    whole_high = whole.astype(BF16)
    whole_low = (whole - whole_high.astype(F32)).astype(BF16)
    gain_rows = jnp.stack([whole_high, whole_low]).reshape(2, groups, width).transpose(1, 0, 2)
    gain_rows = jnp.pad(gain_rows, ((0, 0), (0, 14), (0, 0)))
    expand = (
        lax.broadcasted_iota(jnp.int32, (2 * per, width), 0) % per
        == lax.broadcasted_iota(jnp.int32, (2 * per, width), 1) // size
    ).astype(BF16)

    params = pltpu.CompilerParams(vmem_limit_bytes=VMEM)
    wide = lambda n: pl.BlockSpec((n, width), lambda g: (0, g))
    state_b = lambda n: pl.BlockSpec((n, STATE), lambda g: (0, g))
    state_c = lambda n: pl.BlockSpec((n, STATE), lambda g: (0, g + groups))
    lead = lambda *shape: pl.BlockSpec((1,) + shape, lambda g: (g,) + (0,) * len(shape))
    full = lambda *shape: pl.BlockSpec(shape, lambda g: (0,) * len(shape))
    bias_row = bias_x.reshape(1, inner)
    x_conv, b_conv, c_conv, inc, sums = pl.pallas_call(
        local_kernel,
        grid=(groups,),
        in_specs=[
            wide(rows), wide(RIM), state_b(rows), state_c(rows), state_b(RIM), state_c(RIM),
            wide(4), state_b(4), state_c(4), wide(1), state_b(1), state_c(1),
            full(3, rows, 128), lead(rows, 2 * per), lead(16, width), wide(blocks),
            full(2 * per, width),
        ],
        out_specs=[
            wide(rows), state_b(rows), state_b(rows), lead(STATE, width),
            lead(STATE + 16, width),
        ],
        out_shape=[
            jax.ShapeDtypeStruct((rows, inner), BF16),
            jax.ShapeDtypeStruct((rows, groups * STATE), BF16),
            jax.ShapeDtypeStruct((rows, groups * STATE), BF16),
            jax.ShapeDtypeStruct((groups, STATE, width), F32),
            jax.ShapeDtypeStruct((groups, STATE + 16, width), BF16),
        ],
        scratch_shapes=[
            pltpu.VMEM((rows + RIM, width), F32),
            pltpu.VMEM((rows + RIM, STATE), F32),
            pltpu.VMEM((rows + RIM, STATE), F32),
            pltpu.VMEM((rows, width), BF16),
        ],
        compiler_params=params,
        cost_estimate=pl.CostEstimate(
            flops=4 * rows * inner * STATE, bytes_accessed=30 << 20, transcendentals=rows * inner
        ),
        name="local",
    )(
        x_proj, rim_x, bc_flat, bc_flat, rim_bc, rim_bc, conv_x, wbc, wbc, bias_row, bbc, bbc,
        masks, tail_two, gain_rows, row_gain, expand,
    )

    enter = exchange(sums, groups)

    y = pl.pallas_call(
        intra_kernel,
        grid=(groups,),
        in_specs=[
            wide(rows), state_b(rows), state_b(rows), lead(rows, per),
            lead(blocks, per, STRETCH), full(rows, 1), full(blocks, STRETCH), wide(1),
        ],
        out_specs=wide(rows),
        out_shape=jax.ShapeDtypeStruct((rows, inner), F32),
        compiler_params=params,
        cost_estimate=pl.CostEstimate(
            flops=40 * rows * inner * STRETCH, bytes_accessed=100 << 20,
            transcendentals=rows * heads * STRETCH,
        ),
        name="intra",
    )(
        x_conv, b_conv, c_conv, col, row, seg_ids.reshape(rows, 1), ids,
        jnp.repeat(d_skip, size).reshape(1, inner),
    )

    gated, squares = pl.pallas_call(
        gate_kernel,
        grid=(groups,),
        in_specs=[
            wide(rows), wide(rows), state_b(rows), lead(rows, 2 * per), full(2 * per, width),
            lead(STATE, width), lead(STATE, width), wide(blocks),
        ],
        out_specs=[wide(rows), full(rows, 128)],
        out_shape=[
            jax.ShapeDtypeStruct((rows, inner), F32),
            jax.ShapeDtypeStruct((rows, 128), F32),
        ],
        compiler_params=params,
        name="gate",
    )(y, z_proj, c_conv, link_two, expand, enter, inc, row_gain)

    total = jnp.sum(squares, axis=-1)
    count = lax.axis_size("tp")
    own = total
    for k in range(1, count):
        total = total + lax.ppermute(own, "tp", [(i, (i + k) % count) for i in range(count)])
    scale = lax.rsqrt(total / (inner * count) + 1e-05)
    return (gated * scale[:, None] * norm_gain).astype(BF16)


def solution(mesh):
    in_specs = (
        P("seq", "tp"),
        P("seq", None, "tp"),
        P("seq", "tp"),
        P("seq", "tp"),
        P(None, "tp"),
        P(None, None, "tp"),
        P("tp"),
        P(None, "tp"),
        P("tp"),
        P("tp"),
        P("tp"),
        P("tp"),
        P("seq"),
    )
    return jax.shard_map(
        on_device, mesh=mesh, in_specs=in_specs, out_specs=P("seq", "tp"), check_vma=False
    )
```

time: 533 us -> 108 us (0.20)
  waiting for transfers between devices: 300 us -> 15.4 us
  other arithmetic: 73 us -> 13.8 us
  local copies, waits for them, and re-layouts: 62.1 us -> 14.3 us
  blocking collectives: 43.4 us -> 0 us
  Pallas kernels: 0 us -> 40.7 us
  matrix products: 26.3 us -> 0.4 us
  between operations: 13.8 us -> 0.41 us
  starting transfers between devices: 11.8 us -> 22.5 us
    all_gather x1 -> x0, waiting for transfers between devices: 300 us -> none  [carried_in(): pieces = jax.tree.map(lambda part: lax.all_gather(part, axis), value)]
    all_gather x1 -> x0, blocking collectives: 41 us -> none  [carried_in(): pieces = jax.tree.map(lambda part: lax.all_gather(part, axis), value)]
    pallas_call x0 -> x3, Pallas kernels: none -> 40.7 us  [the longest x1 21 us: on_device(): pl.pallas_call(local_kernel, grid=(groups,), in_specs=[wide(rows), wide(R...]
    select_n x15 -> x0, other arithmetic: 31.1 us -> none  [step(): jnp.where(position < mine, new, old)]
    dot_general x4 -> x1, matrix products: 26.3 us -> 0.4 us  [on_device(): cum = jnp.einsum('ts,csh->cth', tri, logs, precision=lax.Precision.HIGHEST)]
    convert_element_type x7 -> x8, other arithmetic: 31.9 us -> 7.86 us  [the longest x1 6.73 us: on_device(): return (gated * scale[:, None] * norm_gain).astype(BF16)]
    ppermute x3 -> x11, waiting for transfers between devices: 0.01 us -> 15.4 us  [the longest x6 10.3 us: swap(): lax.ppermute(pick(array, place ^ k), axis, [(i, i ^ k) for i in range(cou...]
    unnamed x38 -> x15, local copies, waits for them, and re-layouts: 19.3 us -> 4.59 us
  transfers between devices with their start and end apart: 4 -> 11, of which waited for: 1 -> 7; matrix products, arithmetic and copies ran while one was open for 7% -> 13% of each run, Pallas kernels for 0% -> 9%
where the time goes in v1:
time: 108 us; the launch traced here: 107 us
  Pallas kernels  40.7 us (38%)
  starting transfers between devices  22.5 us (21%)
  waiting for transfers between devices  15.4 us (14%)
  local copies, waits for them, and re-layouts  14.3 us (13%)
  other arithmetic  13.8 us (13%)
    pallas_call x1, Pallas kernels, on_device(): pl.pallas_call(local_kernel, grid=(groups,), in_specs=[wide(rows), wide(R...  21 us
    ppermute x6, waiting for transfers between devices, swap(): lax.ppermute(pick(array, place ^ k), axis, [(i, i ^ k) for i in range(cou...  10.3 us
    pallas_call x1, Pallas kernels, on_device(): pl.pallas_call(gate_kernel, grid=(groups,), in_specs=[wide(rows), wide(ro...  9.85 us
    pallas_call x1, Pallas kernels, on_device(): pl.pallas_call(intra_kernel, grid=(groups,), in_specs=[wide(rows), state_...  9.83 us
    ppermute x6, starting transfers between devices, swap(): lax.ppermute(pick(array, place ^ k), axis, [(i, i ^ k) for i in range(cou...  7.11 us
    convert_element_type x1, other arithmetic, on_device(): return (gated * scale[:, None] * norm_gain).astype(BF16)  6.73 us
    ppermute x1, starting transfers between devices, on_device(): rim_ids = lax.ppermute(seg_ids[rows - RIM:], 'seq', route)  4.83 us
    unnamed x15, local copies, waits for them, and re-layouts  4.59 us
  transfers between devices with their start and end apart: 11, of which 7 were waited for; matrix products, arithmetic and copies ran while one was open for 13% of the time, Pallas kernels for 9%

profile of v1, /device:TPU:0, one launch (start us, length us, event | category | flops | bytes accessed | tf_op | source)
XLA Modules:
  0.0 107.4 jit_solution(8633911106875389299)
XLA Ops:
  0.0 0.8 slice.94
  0.8 4.8 %collective-permute-start.2 = (s32[8]{0:T(128)S(1)}, s32[8]{0:T(128)S(1)}, u32[]{:S(2)}, u32[]{:S(2)}) collective-permute-start(s32[8]{0:T(128)S(1)} %slice.94), channel_id=1, source_target_pairs={{0,2},{2,4},{4,6},{6,8},{8,10},{10,12},{12,14},{14,16},{16,18},{18... | collective-permute-start | bytes 104 | tf_op jit(solution)/shard_map/ppermute | solution.py:217
  5.7 0.7 slice_bitcast_fusion
  6.4 3.4 %collective-permute-start.1 = (bf16[8,1024]{1,0:T(8,128)(2,1)S(1)}, bf16[8,1024]{1,0:T(8,128)(2,1)S(1)}, u32[]{:S(2)}, u32[]{:S(2)}) collective-permute-start(bf16[8,1024]{1,0:T(8,128)(2,1)S(1)} %bitcast.150), channel_id=1, source_target_pairs={{0,2},{2,4},{4,6},{6,8},{8,10},{10,12},{12,14},{14,16},{16,18},{18... | collective-permute-start | bytes 49160 | tf_op jit(solution)/shard_map/ppermute | solution.py:216
  9.8 0.8 slice.91
  10.7 3.4 %collective-permute-start = (bf16[8,4096]{1,0:T(8,128)(2,1)S(1)}, bf16[8,4096]{1,0:T(8,128)(2,1)S(1)}, u32[]{:S(2)}, u32[]{:S(2)}) collective-permute-start(bf16[8,4096]{1,0:T(8,128)(2,1)S(1)} %slice.91), channel_id=1, source_target_pairs={{0,2},{2,4},{4,6},{6,8},{8,10},{10,12},{12,14},{14,16},{16,18},{18... | collective-permute-start | bytes 196616 | tf_op jit(solution)/shard_map/ppermute | solution.py:215
  14.1 0.7 reshape.321.idr_ref
  14.8 0.7 negate_multiply_fusion
  15.5 0.2 slice_reduce_fusion.1
  15.7 0.7 copy.42
  16.4 0.7 copy.41
  17.1 1.1 broadcast_multiply_fusion
  18.1 0.4 convolution_bitcast_fusion
  18.5 0.2 slice_reduce_fusion
  18.7 2.4 %copy.39 = bf16[64,8,2,512]{3,1,2,0:T(8,128)(2,1)} copy(bf16[64,8,2,512]{3,2,1,0:T(2,128)(2,1)} %bitcast.131) | data formatting | bytes 2097152
  21.1 0.1 fusion.22.expand_ref
  21.3 0.1 pad_add_fusion
  21.3 0.1 slice.101
  21.4 0.1 slice_compare_fusion.2
  21.7 0.1 mul.166
  21.9 0.1 mul.167
  22.0 0.1 fusion.15
  22.1 0.1 copy.28
  22.2 0.1 reshape.322
  22.5 0.1 reshape.323.row_gain_ref
  22.6 0.3 copy.29.tail_ref
  22.9 1.2 %broadcast_in_dim.16.masks = f32[3,512,128]{2,1,0:T(8,128)} broadcast(f32[3,512]{1,0:T(4,128)S(1)} %add_convert_fusion), dimensions={0,1} | broadcast | bytes 792576 | tf_op jit(solution)/shard_map/broadcast_in_dim | solution.py:222
  24.1 21.0 %local.1 = (bf16[512,4096]{1,0:T(8,128)(2,1)}, bf16[512,512]{1,0:T(8,128)(2,1)S(1)}, bf16[512,512]{1,0:T(8,128)(2,1)S(1)}, f32[4,128,1024]{2,1,0:T(8,128)}, bf16[4,144,1024]{2,1,0:T(8,128)(2,1)}) custom-call(bf16[512,4096]{1,0:T(8,128)(2,1)} %x_ref.1, bf16[8,4096]{1,0:T(8,128)(2,1)S(1)} %collective-permute-done.rim_ref, bf16[512,1024]{1,0:T(8,128)(2,1)} %bitcast.129, ...), custom_call_target="tpu_custom_call" | custom-call | flops 1073741824 | bytes 31457280 | tf_op jit(solution)/shard_map/local/pallas_call | solution.py:263
  45.1 1.3 %constant_dynamic-slice_fusion.13 = (bf16[1,144,1024]{2,1,0:T(8,128)(2,1)S(1)}, bf16[144,1024]{1,0:T(8,128)(2,1)S(1)}, bf16[144,1024]{1,0:T(8,128)(2,1)S(1)}, bf16[144,1024]{1,0:T(8,128)(2,1)S(1)}) fusion(bf16[4,144,1024]{2,1,0:T(8,128)(2,1)} %get-tuple-element.15, s32[]{:T(128)S(6)} %select_n.61, s32[]{:T(128)S(6)} %select_n.64, s32[]{:T(128)S(6)} %select_n.63, ...), kind=kLoop, calls=%fused_computation.81 | loop fusion | bytes 2359312 | tf_op jit(solution)/shard_map/jit(dynamic_index_in_dim)/dynamic_slice | solution.py:168
  46.4 2.5 %collective-permute-start.5 = (bf16[144,1024]{1,0:T(8,128)(2,1)S(1)}, bf16[144,1024]{1,0:T(8,128)(2,1)}, u32[]{:S(2)}, u32[]{:S(2)}) collective-permute-start(bf16[144,1024]{1,0:T(8,128)(2,1)S(1)} %get-tuple-element.35), channel_id=1, source_target_pairs={{0,6},{2,4},{4,2},{6,0},{8,14},{10,12},{12,10},{14,8},{16,22},{18,... | collective-permute-start | bytes 884744 | tf_op jit(solution)/shard_map/ppermute | solution.py:174
  49.0 0.5 collective-permute-start.4
  49.5 0.5 collective-permute-start.3
  50.0 0.1 copy.30
  50.2 0.1 reshape_reshape.3.skip_ref
  50.3 0.1 reshape.324
  50.4 0.1 copy.34.ids_ref
  50.6 1.4 %copy.31 = f32[512,4,16]{2,0,1:T(8,128)} copy(f32[512,4,16]{0,2,1:T(8,128)S(1)} %reshape.324) | data formatting | bytes 262144 | tf_op jit(solution)/shard_map/reshape | solution.py:238
  52.0 0.1 copy.35
  52.1 0.1 reshape.327
  52.2 5.3 %collective-permute-done.5 = bf16[144,1024]{1,0:T(8,128)(2,1)} collective-permute-done((bf16[144,1024]{1,0:T(8,128)(2,1)S(1)}, bf16[144,1024]{1,0:T(8,128)(2,1)}, u32[]{:S(2)}, u32[]{:S(2)}) %collective-permute-start.5) | collective-permute-done | bytes 294944 | tf_op jit(solution)/shard_map/ppermute | solution.py:174
  57.5 4.2 %collective-permute-done.4 = bf16[144,1024]{1,0:T(8,128)(2,1)} collective-permute-done((bf16[144,1024]{1,0:T(8,128)(2,1)S(1)}, bf16[144,1024]{1,0:T(8,128)(2,1)}, u32[]{:S(2)}, u32[]{:S(2)}) %collective-permute-start.4) | collective-permute-done | bytes 294944 | tf_op jit(solution)/shard_map/ppermute | solution.py:174
  61.7 0.1 collective-permute-done.3
  61.8 1.3 %pad_maximum_fusion = bf16[4,144,1024]{2,1,0:T(8,128)(2,1)S(1)} fusion(bf16[1,144,1024]{2,1,0:T(8,128)(2,1)} %bitcast.15, bf16[1,144,1024]{2,1,0:T(8,128)(2,1)} %bitcast.13, bf16[1,144,1024]{2,1,0:T(8,128)(2,1)} %bitcast.11, bf16[1,144,1024]{2,1,0:T(8,128)(2,1)S(1)} %get-tuple-element.34), kind=kLoop, calls=%fused_computation.1 | loop fusion | flops 1769472 | bytes 2359296 | tf_op jit(solution)/shard_map/stack | solution.py:176
  63.2 0.9 fusion.6
  64.1 3.7 %collective-permute-start.6 = (bf16[128,1024]{1,0:T(8,128)(2,1)}, bf16[128,1024]{1,0:T(8,128)(2,1)S(1)}, u32[]{:S(2)}, u32[]{:S(2)}) collective-permute-start(bf16[128,1024]{1,0:T(8,128)(2,1)} %fusion.6), channel_id=1, source_target_pairs={{0,8},{2,10},{4,12},{6,14},{8,16},{10,18},{12,20},{14,22},{16,24},... | collective-permute-start | bytes 786440 | tf_op jit(solution)/shard_map/ppermute | solution.py:189
  67.8 0.7 pad_maximum_fusion.5
  68.5 1.2 %copy.36.link_ref = bf16[4,512,32]{2,1,0:T(8,128)(2,1)S(1)} copy(bf16[4,512,32]{1,2,0:T(8,128)(2,1)} %pad_maximum_fusion.5) | data formatting | bytes 262144 | tf_op jit(solution)/shard_map/concatenate | solution.py:152
  69.6 3.9 %collective-permute-done.6 = bf16[128,1024]{1,0:T(8,128)(2,1)S(1)} collective-permute-done((bf16[128,1024]{1,0:T(8,128)(2,1)}, bf16[128,1024]{1,0:T(8,128)(2,1)S(1)}, u32[]{:S(2)}, u32[]{:S(2)}) %collective-permute-start.6) | collective-permute-done | bytes 262176 | tf_op jit(solution)/shard_map/ppermute | solution.py:189
  73.5 0.3 fusion.9
  73.8 0.1 pad_maximum_fusion.1
  74.0 0.1 constant_dynamic-slice_fusion.12
  74.1 1.0 collective-permute-start.9
  75.1 2.0 %collective-permute-start.8 = (bf16[128,1024]{1,0:T(8,128)(2,1)S(1)}, bf16[128,1024]{1,0:T(8,128)(2,1)S(1)}, u32[]{:S(2)}, u32[]{:S(2)}) collective-permute-start(bf16[128,1024]{1,0:T(8,128)(2,1)S(1)} %get-tuple-element.44), channel_id=1, source_target_pairs={{0,4},{2,6},{4,0},{6,2},{8,12},{10,14},{12,8},{14,10},{16,20},{18,... | collective-permute-start | bytes 786440 | tf_op jit(solution)/shard_map/ppermute | solution.py:174
  77.1 0.5 collective-permute-start.7
  77.6 9.8 %intra.1.y_ref = f32[512,4096]{1,0:T(8,128)} custom-call(bf16[512,4096]{1,0:T(8,128)(2,1)} %get-tuple-element.12.x_ref, bf16[512,512]{1,0:T(8,128)(2,1)S(1)} %get-tuple-element.13.b_ref, bf16[512,512]{1,0:T(8,128)(2,1)S(1)} %get-tuple-element.14.c_ref, f32[4,512,16]{2,1,0:T(8,128)} %bitcast.132, f32[4,2,16,256]{3,2,1,0:T(8,128)S(1)} %bitcast.123, ...), custom_call_target="tpu_custom_call" | custom-call | flops 21474836480 | bytes 104857600 | tf_op jit(solution)/shard_map/intra/pallas_call | solution.py:301
  87.5 0.5 collective-permute-done.8
  87.9 0.2 collective-permute-done.7
  88.1 0.1 pad_maximum_fusion.2
  88.3 0.1 constant_dynamic-slice_fusion.11
  88.4 1.1 %pad_maximum_fusion.3.enter_ref = bf16[4,128,1024]{2,1,0:T(8,128)(2,1)} fusion(bf16[1,128,1024]{2,1,0:T(8,128)(2,1)S(1)} %get-tuple-element.39, bf16[1,128,1024]{2,1,0:T(8,128)(2,1)S(1)} %get-tuple-element.40, bf16[1,128,1024]{2,1,0:T(8,128)(2,1)S(1)} %get-tuple-element.41, bf16[1,128,1024]{2,1,0:T(8,128)(2,1)S(1)} %get-tuple-element.38), kind=kLoop, calls=%fused_computation.5 | loop fusion | flops 1572864 | bytes 2097152 | tf_op jit(solution)/shard_map/stack | solution.py:194
  89.5 9.8 %gate.1 = (f32[512,4096]{1,0:T(8,128)}, f32[512,128]{1,0:T(8,128)S(1)}) custom-call(f32[512,4096]{1,0:T(8,128)} %intra.1.y_ref, bf16[512,4096]{1,0:T(8,128)(2,1)} %z_ref.1, bf16[512,512]{1,0:T(8,128)(2,1)S(1)} %get-tuple-element.14.c_ref, bf16[4,512,32]{2,1,0:T(8,128)(2,1)S(1)} %copy.36.link_ref, bf16[32,1024]{1,0:T(8,128)(2,1)S(1)} %fusion.22.expand_ref, ...), custom_call_target="tpu_custom_call" | custom-call | tf_op jit(solution)/shard_map/gate/pallas_call | solution.py:321
  99.3 0.1 reduce_sum.9
  99.5 1.1 %collective-permute-done.10 = f32[512]{0:T(512)S(1)} collective-permute-done((f32[512]{0:T(512)S(1)}, f32[512]{0:T(512)S(1)}, u32[]{:S(2)}, u32[]{:S(2)}) %collective-permute-start.10) | collective-permute-done | bytes 2080 | tf_op jit(solution)/shard_map/ppermute | solution.py:341
  100.7 6.7 %multiply_convert_fusion = bf16[512,4096]{1,0:T(8,128)(2,1)} fusion(f32[512,4096]{1,0:T(8,128)} %get-tuple-element.17, f32[4096]{0:T(1024)S(1)} %copy-done.3, f32[512]{0:T(512)S(1)} %add_rsqrt_fusion), kind=kLoop, calls=%fused_computation | loop fusion | flops 6291456 | bytes 12601344 | tf_op jit(solution)/shard_map/convert_element_type | solution.py:343
  (41 shorter events, 0.7 us)
Async XLA Ops:
  0.0 21.2 %copy-start.2 = (s32[512]{0:T(512)S(1)}, s32[512]{0:T(512)}, u32[]{:S(2)}) copy-start(s32[512]{0:T(512)} %param.25) | copy-start | bytes 6148
  0.8 20.4 %collective-permute-start.2 = (s32[8]{0:T(128)S(1)}, s32[8]{0:T(128)S(1)}, u32[]{:S(2)}, u32[]{:S(2)}) collective-permute-start(s32[8]{0:T(128)S(1)} %slice.94), channel_id=1, source_target_pairs={{0,2},{2,4},{4,6},{6,8},{8,10},{10,12},{12,14},{14,16},{16,18},{18... | collective-permute-start | bytes 104 | tf_op jit(solution)/shard_map/ppermute | solution.py:217
  6.4 16.5 %collective-permute-start.1 = (bf16[8,1024]{1,0:T(8,128)(2,1)S(1)}, bf16[8,1024]{1,0:T(8,128)(2,1)S(1)}, u32[]{:S(2)}, u32[]{:S(2)}) collective-permute-start(bf16[8,1024]{1,0:T(8,128)(2,1)S(1)} %bitcast.150), channel_id=1, source_target_pairs={{0,2},{2,4},{4,6},{6,8},{8,10},{10,12},{12,14},{14,16},{16,18},{18... | collective-permute-start | bytes 49160 | tf_op jit(solution)/shard_map/ppermute | solution.py:216
  10.7 12.3 %collective-permute-start = (bf16[8,4096]{1,0:T(8,128)(2,1)S(1)}, bf16[8,4096]{1,0:T(8,128)(2,1)S(1)}, u32[]{:S(2)}, u32[]{:S(2)}) collective-permute-start(bf16[8,4096]{1,0:T(8,128)(2,1)S(1)} %slice.91), channel_id=1, source_target_pairs={{0,2},{2,4},{4,6},{6,8},{8,10},{10,12},{12,14},{14,16},{16,18},{18... | collective-permute-start | bytes 196616 | tf_op jit(solution)/shard_map/ppermute | solution.py:215
  21.1 3.0 %copy-start = (bf16[4,4096]{1,0:T(4,128)(2,1)S(1)}, bf16[4,4096]{1,0:T(4,128)(2,1)}, u32[]{:S(2)}) copy-start(bf16[4,4096]{1,0:T(4,128)(2,1)} %wx_ref.1) | copy-start | bytes 98308
  21.1 3.0 %copy-start.1 = (f32[4096]{0:T(1024)S(1)}, f32[4096]{0:T(1024)}, u32[]{:S(2)}) copy-start(f32[4096]{0:T(1024)} %param.19) | copy-start | bytes 49156
  45.1 5.0 %copy-start.4 = (f32[64]{0:T(128)S(1)}, f32[64]{0:T(128)}, u32[]{:S(2)}) copy-start(f32[64]{0:T(128)} %param.23) | copy-start | bytes 772
  46.4 11.1 %collective-permute-start.5 = (bf16[144,1024]{1,0:T(8,128)(2,1)S(1)}, bf16[144,1024]{1,0:T(8,128)(2,1)}, u32[]{:S(2)}, u32[]{:S(2)}) collective-permute-start(bf16[144,1024]{1,0:T(8,128)(2,1)S(1)} %get-tuple-element.35), channel_id=1, source_target_pairs={{0,6},{2,4},{4,2},{6,0},{8,14},{10,12},{12,10},{14,8},{16,22},{18,... | collective-permute-start | bytes 884744 | tf_op jit(solution)/shard_map/ppermute | solution.py:174
  49.0 12.8 %collective-permute-start.4 = (bf16[144,1024]{1,0:T(8,128)(2,1)S(1)}, bf16[144,1024]{1,0:T(8,128)(2,1)}, u32[]{:S(2)}, u32[]{:S(2)}) collective-permute-start(bf16[144,1024]{1,0:T(8,128)(2,1)S(1)} %get-tuple-element.36), channel_id=1, source_target_pairs={{0,4},{2,6},{4,0},{6,2},{8,12},{10,14},{12,8},{14,10},{16,20},{18,... | collective-permute-start | bytes 884744 | tf_op jit(solution)/shard_map/ppermute | solution.py:174
  49.5 12.4 %collective-permute-start.3 = (bf16[144,1024]{1,0:T(8,128)(2,1)S(1)}, bf16[144,1024]{1,0:T(8,128)(2,1)}, u32[]{:S(2)}, u32[]{:S(2)}) collective-permute-start(bf16[144,1024]{1,0:T(8,128)(2,1)S(1)} %get-tuple-element.37), channel_id=1, source_target_pairs={{0,2},{2,0},{4,6},{6,4},{8,10},{10,8},{12,14},{14,12},{16,18},{18,... | collective-permute-start | bytes 884744 | tf_op jit(solution)/shard_map/ppermute | solution.py:174
  64.1 9.4 %collective-permute-start.6 = (bf16[128,1024]{1,0:T(8,128)(2,1)}, bf16[128,1024]{1,0:T(8,128)(2,1)S(1)}, u32[]{:S(2)}, u32[]{:S(2)}) collective-permute-start(bf16[128,1024]{1,0:T(8,128)(2,1)} %fusion.6), channel_id=1, source_target_pairs={{0,8},{2,10},{4,12},{6,14},{8,16},{10,18},{12,20},{14,22},{16,24},... | collective-permute-start | bytes 786440 | tf_op jit(solution)/shard_map/ppermute | solution.py:189
  74.1 13.4 %collective-permute-start.9 = (bf16[128,1024]{1,0:T(8,128)(2,1)S(1)}, bf16[128,1024]{1,0:T(8,128)(2,1)S(1)}, u32[]{:S(2)}, u32[]{:S(2)}) collective-permute-start(bf16[128,1024]{1,0:T(8,128)(2,1)S(1)} %get-tuple-element.43), channel_id=1, source_target_pairs={{0,6},{2,4},{4,2},{6,0},{8,14},{10,12},{12,10},{14,8},{16,22},{18,... | collective-permute-start | bytes 786440 | tf_op jit(solution)/shard_map/ppermute | solution.py:174
  75.1 12.8 %collective-permute-start.8 = (bf16[128,1024]{1,0:T(8,128)(2,1)S(1)}, bf16[128,1024]{1,0:T(8,128)(2,1)S(1)}, u32[]{:S(2)}, u32[]{:S(2)}) collective-permute-start(bf16[128,1024]{1,0:T(8,128)(2,1)S(1)} %get-tuple-element.44), channel_id=1, source_target_pairs={{0,4},{2,6},{4,0},{6,2},{8,12},{10,14},{12,8},{14,10},{16,20},{18,... | collective-permute-start | bytes 786440 | tf_op jit(solution)/shard_map/ppermute | solution.py:174
  77.1 11.0 %collective-permute-start.7 = (bf16[128,1024]{1,0:T(8,128)(2,1)S(1)}, bf16[128,1024]{1,0:T(8,128)(2,1)S(1)}, u32[]{:S(2)}, u32[]{:S(2)}) collective-permute-start(bf16[128,1024]{1,0:T(8,128)(2,1)S(1)} %get-tuple-element.45), channel_id=1, source_target_pairs={{0,2},{2,0},{4,6},{6,4},{8,10},{10,8},{12,14},{14,12},{16,18},{18,... | collective-permute-start | bytes 786440 | tf_op jit(solution)/shard_map/ppermute | solution.py:174
  89.5 11.2 %copy-start.3 = (f32[4096]{0:T(1024)S(1)}, f32[4096]{0:T(1024)}, u32[]{:S(2)}) copy-start(f32[4096]{0:T(1024)} %param.24) | copy-start | bytes 49156
  99.5 1.2 %collective-permute-start.10 = (f32[512]{0:T(512)S(1)}, f32[512]{0:T(512)S(1)}, u32[]{:S(2)}, u32[]{:S(2)}) collective-permute-start(f32[512]{0:T(512)S(1)} %reduce_sum.9), channel_id=1, source_target_pairs={{0,1},{1,0},{2,3},{3,2},{4,5},{5,4},{6,7},{7,6},{8,9},{9,8},{10,11... | collective-permute-start | bytes 6152 | tf_op jit(solution)/shard_map/ppermute | solution.py:341

commit v2 on v1

--- a/solution.py
+++ b/solution.py
@@ -1,3 +1,5 @@
+import functools
+
 import jax
 import jax.numpy as jnp
 from jax import lax
@@ -19,10 +21,10 @@
     return half * jnp.tanh(half) + half
 
 
-def conv_tile(window, weight, bias, masks, start, rows, lanes):
-    acc = jnp.broadcast_to(bias, (rows, lanes.stop - lanes.start))
+def conv_tile(window, weight, bias, masks, start, rows):
+    acc = jnp.broadcast_to(bias, (rows, 128))
     for tap in range(4):
-        piece = window[pl.ds(RIM - 3 + tap + start, rows), lanes]
+        piece = window[pl.ds(RIM - 3 + tap + start, rows), :]
         term = piece * weight[tap : tap + 1]
         if tap < 3:
             term = term * masks[tap, pl.ds(start, rows), :]
@@ -32,32 +34,39 @@
 
 def local_kernel(
     x_ref, rim_ref, b_ref, c_ref, rimb_ref, rimc_ref, wx_ref, wb_ref, wc_ref,
-    bx_ref, bb_ref, bc_ref, masks, tail_ref, gain_ref, row_gain_ref, expand_ref,
-    xo_ref, bo_ref, co_ref, inc_ref, sum_ref, window, window_b, window_c, weighted,
+    bx_ref, bb_ref, bc_ref, counted_ref, tail_ref, gain_ref, row_gain_ref, expand_ref,
+    xo_ref, bo_ref, co_ref, inc_ref, sum_ref, window, window_b, window_c, weighted, masks,
 ):
     rows, width = x_ref.shape
     blocks = rows // STRETCH
-    window[0:RIM] = rim_ref[...].astype(F32)
+
+    @pl.when(pl.program_id(0) == 0)
+    def _():
+        for tap in range(3):
+            masks[tap] = jnp.broadcast_to(counted_ref[:, tap : tap + 1], (rows, 128))
+
     window_b[0:RIM] = rimb_ref[...].astype(F32)
     window_c[0:RIM] = rimc_ref[...].astype(F32)
     window_b[RIM:] = b_ref[...].astype(F32)
     window_c[RIM:] = c_ref[...].astype(F32)
-    one = slice(0, STATE)
     for block in range(blocks):
         at = slice(block * STRETCH, (block + 1) * STRETCH)
         bo_ref[at] = conv_tile(
-            window_b, wb_ref[...].astype(F32), bb_ref[...], masks, at.start, STRETCH, one
+            window_b, wb_ref[...].astype(F32), bb_ref[...], masks, at.start, STRETCH
         )
         co_ref[at] = conv_tile(
-            window_c, wc_ref[...].astype(F32), bc_ref[...], masks, at.start, STRETCH, one
+            window_c, wc_ref[...].astype(F32), bc_ref[...], masks, at.start, STRETCH
         )
     for tile in range(width // 128):
         lanes = slice(tile * 128, (tile + 1) * 128)
-        window[RIM:, lanes] = x_ref[:, lanes].astype(F32)
+        window[tile, 0:RIM] = rim_ref[:, lanes].astype(F32)
+        window[tile, RIM:] = x_ref[:, lanes].astype(F32)
         weight = wx_ref[:, lanes].astype(F32)
         for block in range(blocks):
             at = slice(block * STRETCH, (block + 1) * STRETCH)
-            value = conv_tile(window, weight, bx_ref[:, lanes], masks, at.start, STRETCH, lanes)
+            value = conv_tile(
+                window.at[tile], weight, bx_ref[:, lanes], masks, at.start, STRETCH
+            )
             xo_ref[at, lanes] = value
             spread = jnp.dot(
                 tail_ref[0, at, :], expand_ref[:, lanes], preferred_element_type=F32
@@ -147,6 +156,11 @@
             sq_ref[at] += square[:, :128] + square[:, 128:]
 
 
+def norm_kernel(gated_ref, total_ref, gain_ref, out_ref, *, channels):
+    scale = lax.rsqrt(total_ref[...] / channels + 1e-05)
+    out_ref[...] = (gated_ref[...] * scale * gain_ref[...]).astype(BF16)
+
+
 def split_two(value):
     high = value.astype(BF16)
     return jnp.concatenate([high, (value - high.astype(F32)).astype(BF16)], axis=-1)
@@ -212,14 +226,19 @@
     wbc = conv_bc.reshape(4, 2 * groups * STATE)
     bbc = bias_bc.reshape(1, 2 * groups * STATE)
     route = [(i, i + 1) for i in range(seq - 1)]
-    rim_x = lax.ppermute(x_proj[rows - RIM :], "seq", route)
-    rim_bc = lax.ppermute(bc_flat[rows - RIM :], "seq", route)
-    rim_ids = lax.ppermute(seg_ids[rows - RIM :], "seq", route)
+    tail_ids = jnp.broadcast_to(seg_ids[rows - RIM :, None], (RIM, 128)).astype(BF16)
+    ends = [
+        x_proj[rows - RIM :],
+        bc_proj[rows - RIM :].reshape(RIM, 2 * groups * STATE),
+        tail_ids,
+    ]
+    rim = lax.ppermute(jnp.concatenate(ends, axis=1), "seq", route)
+    rim_ids = rim[:, inner + 2 * groups * STATE].astype(jnp.int32)
     window_ids = jnp.concatenate([rim_ids, seg_ids])
-    masks = jnp.stack(
-        [(window_ids[RIM - 3 + k : RIM - 3 + k + rows] == seg_ids).astype(F32) for k in range(3)]
-    )
-    masks = jnp.broadcast_to(masks[:, :, None], (3, rows, 128))
+    counted = jnp.stack(
+        [(window_ids[RIM - 3 + k : RIM - 3 + k + rows] == seg_ids).astype(F32) for k in range(3)],
+        axis=1,
+    )
 
     step = jax.nn.softplus(dt_raw + dt_bias)
     rate = -jnp.exp(a_log) * LOG2E
@@ -258,15 +277,18 @@
     state_b = lambda n: pl.BlockSpec((n, STATE), lambda g: (0, g))
     state_c = lambda n: pl.BlockSpec((n, STATE), lambda g: (0, g + groups))
     lead = lambda *shape: pl.BlockSpec((1,) + shape, lambda g: (g,) + (0,) * len(shape))
+    tiles = inner // STATE
+    rim_b = pl.BlockSpec((RIM, STATE), lambda g: (0, tiles + g))
+    rim_c = pl.BlockSpec((RIM, STATE), lambda g: (0, tiles + groups + g))
     full = lambda *shape: pl.BlockSpec(shape, lambda g: (0,) * len(shape))
     bias_row = bias_x.reshape(1, inner)
     x_conv, b_conv, c_conv, inc, sums = pl.pallas_call(
         local_kernel,
         grid=(groups,),
         in_specs=[
-            wide(rows), wide(RIM), state_b(rows), state_c(rows), state_b(RIM), state_c(RIM),
+            wide(rows), wide(RIM), state_b(rows), state_c(rows), rim_b, rim_c,
             wide(4), state_b(4), state_c(4), wide(1), state_b(1), state_c(1),
-            full(3, rows, 128), lead(rows, 2 * per), lead(16, width), wide(blocks),
+            full(rows, 3), lead(rows, 2 * per), lead(16, width), wide(blocks),
             full(2 * per, width),
         ],
         out_specs=[
@@ -281,10 +303,11 @@
             jax.ShapeDtypeStruct((groups, STATE + 16, width), BF16),
         ],
         scratch_shapes=[
-            pltpu.VMEM((rows + RIM, width), F32),
+            pltpu.VMEM((width // 128, rows + RIM, 128), F32),
             pltpu.VMEM((rows + RIM, STATE), F32),
             pltpu.VMEM((rows + RIM, STATE), F32),
             pltpu.VMEM((rows, width), BF16),
+            pltpu.VMEM((3, rows, 128), F32),
         ],
         compiler_params=params,
         cost_estimate=pl.CostEstimate(
@@ -292,8 +315,8 @@
         ),
         name="local",
     )(
-        x_proj, rim_x, bc_flat, bc_flat, rim_bc, rim_bc, conv_x, wbc, wbc, bias_row, bbc, bbc,
-        masks, tail_two, gain_rows, row_gain, expand,
+        x_proj, rim, bc_flat, bc_flat, rim, rim, conv_x, wbc, wbc, bias_row, bbc, bbc,
+        counted, tail_two, gain_rows, row_gain, expand,
     )
 
     enter = exchange(sums, groups)
@@ -334,13 +357,25 @@
         name="gate",
     )(y, z_proj, c_conv, link_two, expand, enter, inc, row_gain)
 
-    total = jnp.sum(squares, axis=-1)
+    total = jnp.sum(squares, axis=-1, keepdims=True)
     count = lax.axis_size("tp")
     own = total
     for k in range(1, count):
         total = total + lax.ppermute(own, "tp", [(i, (i + k) % count) for i in range(count)])
-    scale = lax.rsqrt(total / (inner * count) + 1e-05)
-    return (gated * scale[:, None] * norm_gain).astype(BF16)
+    part = rows // 4
+    return pl.pallas_call(
+        functools.partial(norm_kernel, channels=inner * count),
+        grid=(4,),
+        in_specs=[
+            pl.BlockSpec((part, inner), lambda r: (r, 0)),
+            pl.BlockSpec((part, 1), lambda r: (r, 0)),
+            full(1, inner),
+        ],
+        out_specs=pl.BlockSpec((part, inner), lambda r: (r, 0)),
+        out_shape=jax.ShapeDtypeStruct((rows, inner), BF16),
+        compiler_params=params,
+        name="norm",
+    )(gated, total, norm_gain.reshape(1, inner))
 
 
 def solution(mesh):

time: 108 us -> 98.4 us (0.911)
  waiting for transfers between devices: 15.4 us -> 22.8 us
  starting transfers between devices: 22.5 us -> 15.4 us
  other arithmetic: 13.8 us -> 7.37 us
  Pallas kernels: 40.7 us -> 38.4 us
  local copies, waits for them, and re-layouts: 14.3 us -> 13 us
    ppermute x6, waiting for transfers between devices: 10.3 us -> 21.3 us  [swap(): lax.ppermute(pick(array, place ^ k), axis, [(i, i ^ k) for i in range(cou...]
    pallas_call x1, Pallas kernels: 21 us -> 12.4 us  [on_device(): pl.pallas_call(local_kernel, grid=(groups,), in_specs=[wide(rows), wide(R...]
    ppermute x3 -> x1, starting transfers between devices: 11.6 us -> 4.84 us  [on_device(): rim = lax.ppermute(jnp.concatenate(ends, axis=1), 'seq', route)]
    convert_element_type x1, other arithmetic: 6.73 us -> 0.12 us  [on_device(): rim_ids = rim[:, inner + 2 * groups * STATE].astype(jnp.int32)]
    pallas_call x0 -> x1, Pallas kernels: none -> 6.12 us  [on_device(): pl.pallas_call(functools.partial(norm_kernel, channels=inner * count), gr...]
    ppermute x1, waiting for transfers between devices: 3.89 us -> 0.01 us  [exchange(): lax.ppermute(run.astype(BF16), axis, [(i, i + plane) for i in range(count...]
    unnamed x15 -> x23, local copies, waits for them, and re-layouts: 4.59 us -> 4.09 us
  transfers between devices with their start and end apart: 11 -> 9, of which waited for: 7 -> 7; matrix products, arithmetic and copies ran while one was open for 13% -> 8% of each run, Pallas kernels for 9% -> 10%
where the time goes in v2:
time: 98.4 us; the launch traced here: 97.8 us
  Pallas kernels  38.4 us (39%)
  waiting for transfers between devices  22.8 us (23%)
  starting transfers between devices  15.4 us (16%)
  local copies, waits for them, and re-layouts  13 us (13%)
  other arithmetic  7.37 us (7%)
    ppermute x6, waiting for transfers between devices, swap(): lax.ppermute(pick(array, place ^ k), axis, [(i, i ^ k) for i in range(cou...  21.3 us
    pallas_call x1, Pallas kernels, on_device(): pl.pallas_call(local_kernel, grid=(groups,), in_specs=[wide(rows), wide(R...  12.4 us
    pallas_call x1, Pallas kernels, on_device(): pl.pallas_call(gate_kernel, grid=(groups,), in_specs=[wide(rows), wide(ro...  9.99 us
    pallas_call x1, Pallas kernels, on_device(): pl.pallas_call(intra_kernel, grid=(groups,), in_specs=[wide(rows), state_...  9.92 us
    ppermute x6, starting transfers between devices, swap(): lax.ppermute(pick(array, place ^ k), axis, [(i, i ^ k) for i in range(cou...  7.04 us
    pallas_call x1, Pallas kernels, on_device(): pl.pallas_call(functools.partial(norm_kernel, channels=inner * count), gr...  6.12 us
    ppermute x1, starting transfers between devices, on_device(): rim = lax.ppermute(jnp.concatenate(ends, axis=1), 'seq', route)  4.84 us
    unnamed x23, local copies, waits for them, and re-layouts  4.09 us
  transfers between devices with their start and end apart: 9, of which 7 were waited for; matrix products, arithmetic and copies ran while one was open for 8% of the time, Pallas kernels for 10%

profile of v2, /device:TPU:0, one launch (start us, length us, event | category | flops | bytes accessed | tf_op | source)
XLA Modules:
  0.0 97.8 jit_solution(10505790289711553007)
XLA Ops:
  0.0 0.8 convert.12
  0.8 0.1 slice.94
  0.9 0.7 slice_bitcast_fusion
  1.6 0.8 slice.92
  2.5 4.8 %collective-permute-start = (bf16[8,5248]{1,0:T(8,128)(2,1)S(1)}, bf16[8,5248]{1,0:T(8,128)(2,1)S(1)}, u32[]{:S(2)}, u32[]{:S(2)}) collective-permute-start(bf16[8,5248]{1,0:T(8,128)(2,1)S(1)} %pad_maximum_fusion.6), channel_id=1, source_target_pairs={{0,2},{2,4},{4,6},{6,8},{8,10},{10,12},{12,14},{14,16},{16,18},{18... | collective-permute-start | bytes 251912 | tf_op jit(solution)/shard_map/ppermute | solution.py:235
  7.4 0.7 reshape.327.idr_ref
  8.1 0.7 negate_multiply_fusion
  8.8 0.7 copy.64
  9.5 0.7 copy.63
  10.2 1.1 %broadcast_multiply_fusion = (f32[512,64]{0,1:T(8,128)S(1)}, f32[512,64]{0,1:T(8,128)S(1)}) fusion(f32[64]{0:T(128)S(1)} %negate_multiply_fusion, f32[512,64]{0,1:T(8,128)} %param.16, f32[64]{0:T(128)} %param.21), kind=kLoop, calls=%fused_computation.60 | loop fusion | flops 262144 | bytes 393728 | tf_op jit(solution)/shard_map/mul | solution.py:246
  11.3 0.4 convolution_bitcast_fusion
  11.7 0.2 slice_reduce_fusion
  11.8 1.2 %copy.62 = bf16[64,8,2,512]{3,1,2,0:T(8,128)(2,1)} copy(bf16[64,8,2,512]{3,2,1,0:T(2,128)(2,1)S(1)} %bitcast.134) | data formatting | bytes 2097152
  13.1 0.1 fusion.22.expand_ref
  13.1 0.2 slice_reduce_fusion.1
  13.3 0.1 convert_reduce_fusion
  13.5 0.1 slice.102
  13.8 0.1 copy.48.counted_ref
  14.1 0.1 mul.150
  14.2 0.1 mul.151
  14.4 0.1 reshape.329.row_gain_ref
  14.6 0.1 fusion.15
  14.7 0.1 copy.47
  14.8 0.1 reshape.328
  14.9 1.0 %copy.49.tail_ref = bf16[4,512,32]{2,1,0:T(8,128)(2,1)} copy(bf16[4,512,32]{1,2,0:T(8,128)(2,1)S(1)} %pad_maximum_fusion.4) | data formatting | bytes 262144 | tf_op jit(solution)/shard_map/concatenate | solution.py:166
  16.1 12.4 %local.1 = (bf16[512,4096]{1,0:T(8,128)(2,1)}, bf16[512,512]{1,0:T(8,128)(2,1)S(1)}, bf16[512,512]{1,0:T(8,128)(2,1)S(1)}, f32[4,128,1024]{2,1,0:T(8,128)}, bf16[4,144,1024]{2,1,0:T(8,128)(2,1)}) custom-call(bf16[512,4096]{1,0:T(8,128)(2,1)} %x_ref.1, bf16[8,5248]{1,0:T(8,128)(2,1)S(1)} %collective-permute-done.rim_ref.rimb_ref.rimc_ref, ...), custom_call_target="tpu_custom_call" | custom-call | flops 1073741824 | bytes 31457280 | tf_op jit(solution)/shard_map/local/pallas_call | solution.py:285
  28.4 2.2 %constant_dynamic-slice_fusion.13 = (bf16[1,144,1024]{2,1,0:T(8,128)(2,1)S(1)}, bf16[144,1024]{1,0:T(8,128)(2,1)}, bf16[144,1024]{1,0:T(8,128)(2,1)}, bf16[144,1024]{1,0:T(8,128)(2,1)S(1)}) fusion(bf16[4,144,1024]{2,1,0:T(8,128)(2,1)} %get-tuple-element.15, s32[]{:T(128)S(6)} %select_n.61, s32[]{:T(128)S(6)} %select_n.64, s32[]{:T(128)S(6)} %select_n.63, ...), kind=kLoop, calls=%fused_computation.81 | loop fusion | bytes 2359312 | tf_op jit(solution)/shard_map/jit(dynamic_index_in_dim)/dynamic_slice | solution.py:182
  30.6 2.5 %collective-permute-start.3 = (bf16[144,1024]{1,0:T(8,128)(2,1)}, bf16[144,1024]{1,0:T(8,128)(2,1)S(1)}, u32[]{:S(2)}, u32[]{:S(2)}) collective-permute-start(bf16[144,1024]{1,0:T(8,128)(2,1)} %get-tuple-element.35), channel_id=1, source_target_pairs={{0,6},{2,4},{4,2},{6,0},{8,14},{10,12},{12,10},{14,8},{16,22},{18,... | collective-permute-start | bytes 884744 | tf_op jit(solution)/shard_map/ppermute | solution.py:188
  33.1 0.5 collective-permute-start.2
  33.6 0.5 collective-permute-start.1
  34.1 0.1 copy.50
  34.3 0.1 reshape_reshape.3.skip_ref
  34.4 0.1 reshape.330
  34.5 0.1 copy.54.ids_ref
  34.7 1.4 %copy.51 = f32[512,4,16]{2,0,1:T(8,128)} copy(f32[512,4,16]{0,2,1:T(8,128)S(1)} %reshape.330) | data formatting | bytes 262144 | tf_op jit(solution)/shard_map/reshape | solution.py:257
  36.1 5.6 %collective-permute-done.3 = bf16[144,1024]{1,0:T(8,128)(2,1)S(1)} collective-permute-done((bf16[144,1024]{1,0:T(8,128)(2,1)}, bf16[144,1024]{1,0:T(8,128)(2,1)S(1)}, u32[]{:S(2)}, u32[]{:S(2)}) %collective-permute-start.3) | collective-permute-done | bytes 294944 | tf_op jit(solution)/shard_map/ppermute | solution.py:188
  41.7 4.8 %collective-permute-done.2 = bf16[144,1024]{1,0:T(8,128)(2,1)S(1)} collective-permute-done((bf16[144,1024]{1,0:T(8,128)(2,1)}, bf16[144,1024]{1,0:T(8,128)(2,1)S(1)}, u32[]{:S(2)}, u32[]{:S(2)}) %collective-permute-start.2) | collective-permute-done | bytes 294944 | tf_op jit(solution)/shard_map/ppermute | solution.py:188
  46.5 0.1 collective-permute-done.1
  46.6 0.6 copy-done.5
  47.2 0.1 copy-done.6
  47.3 1.3 %pad_maximum_fusion = bf16[4,144,1024]{2,1,0:T(8,128)(2,1)S(1)} fusion(bf16[1,144,1024]{2,1,0:T(8,128)(2,1)} %bitcast.140, bf16[1,144,1024]{2,1,0:T(8,128)(2,1)} %bitcast.141, bf16[1,144,1024]{2,1,0:T(8,128)(2,1)} %bitcast.142, bf16[1,144,1024]{2,1,0:T(8,128)(2,1)S(1)} %get-tuple-element.34), kind=kLoop, calls=%fused_computation | loop fusion | flops 1769472 | bytes 2359296 | tf_op jit(solution)/shard_map/stack | solution.py:190
  48.7 0.9 fusion.6
  49.6 3.5 %collective-permute-start.4 = (bf16[128,1024]{1,0:T(8,128)(2,1)}, bf16[128,1024]{1,0:T(8,128)(2,1)S(1)}, u32[]{:S(2)}, u32[]{:S(2)}) collective-permute-start(bf16[128,1024]{1,0:T(8,128)(2,1)} %fusion.6), channel_id=1, source_target_pairs={{0,8},{2,10},{4,12},{6,14},{8,16},{10,18},{12,20},{14,22},{16,24},... | collective-permute-start | bytes 786440 | tf_op jit(solution)/shard_map/ppermute | solution.py:203
  53.1 9.9 %intra.1.y_ref = f32[512,4096]{1,0:T(8,128)} custom-call(bf16[512,4096]{1,0:T(8,128)(2,1)} %get-tuple-element.12.x_ref, bf16[512,512]{1,0:T(8,128)(2,1)S(1)} %get-tuple-element.13.b_ref, bf16[512,512]{1,0:T(8,128)(2,1)S(1)} %get-tuple-element.14.c_ref, f32[4,512,16]{2,1,0:T(8,128)} %bitcast.135, f32[4,2,16,256]{3,2,1,0:T(8,128)S(1)} %bitcast.125, ...), custom_call_target="tpu_custom_call" | custom-call | flops 21474836480 | bytes 104857600 | tf_op jit(solution)/shard_map/intra/pallas_call | solution.py:324
  63.0 0.1 copy.55
  63.1 0.1 reshape.333
  63.3 0.3 fusion.9
  63.6 0.1 pad_maximum_fusion.1
  63.7 0.1 constant_dynamic-slice_fusion.12
  63.8 1.8 %collective-permute-start.7 = (bf16[128,1024]{1,0:T(8,128)(2,1)S(1)}, bf16[128,1024]{1,0:T(8,128)(2,1)S(1)}, u32[]{:S(2)}, u32[]{:S(2)}) collective-permute-start(bf16[128,1024]{1,0:T(8,128)(2,1)S(1)} %get-tuple-element.43), channel_id=1, source_target_pairs={{0,6},{2,4},{4,2},{6,0},{8,14},{10,12},{12,10},{14,8},{16,22},{18,... | collective-permute-start | bytes 786440 | tf_op jit(solution)/shard_map/ppermute | solution.py:188
  65.6 1.2 %collective-permute-start.6 = (bf16[128,1024]{1,0:T(8,128)(2,1)S(1)}, bf16[128,1024]{1,0:T(8,128)(2,1)S(1)}, u32[]{:S(2)}, u32[]{:S(2)}) collective-permute-start(bf16[128,1024]{1,0:T(8,128)(2,1)S(1)} %get-tuple-element.44), channel_id=1, source_target_pairs={{0,4},{2,6},{4,0},{6,2},{8,12},{10,14},{12,8},{14,10},{16,20},{18,... | collective-permute-start | bytes 786440 | tf_op jit(solution)/shard_map/ppermute | solution.py:188
  66.8 0.5 collective-permute-start.5
  67.4 0.3 copy.56.link_ref
  67.7 6.3 %collective-permute-done.7 = bf16[128,1024]{1,0:T(8,128)(2,1)S(1)} collective-permute-done((bf16[128,1024]{1,0:T(8,128)(2,1)S(1)}, bf16[128,1024]{1,0:T(8,128)(2,1)S(1)}, u32[]{:S(2)}, u32[]{:S(2)}) %collective-permute-start.7) | collective-permute-done | bytes 262176 | tf_op jit(solution)/shard_map/ppermute | solution.py:188
  74.0 4.3 %collective-permute-done.6 = bf16[128,1024]{1,0:T(8,128)(2,1)S(1)} collective-permute-done((bf16[128,1024]{1,0:T(8,128)(2,1)S(1)}, bf16[128,1024]{1,0:T(8,128)(2,1)S(1)}, u32[]{:S(2)}, u32[]{:S(2)}) %collective-permute-start.6) | collective-permute-done | bytes 262176 | tf_op jit(solution)/shard_map/ppermute | solution.py:188
  78.3 0.1 collective-permute-done.5
  78.4 0.1 pad_maximum_fusion.2
  78.6 0.1 constant_dynamic-slice_fusion.11
  78.7 1.1 %pad_maximum_fusion.3.enter_ref = bf16[4,128,1024]{2,1,0:T(8,128)(2,1)} fusion(bf16[1,128,1024]{2,1,0:T(8,128)(2,1)S(1)} %get-tuple-element.39, bf16[1,128,1024]{2,1,0:T(8,128)(2,1)S(1)} %get-tuple-element.40, bf16[1,128,1024]{2,1,0:T(8,128)(2,1)S(1)} %get-tuple-element.41, bf16[1,128,1024]{2,1,0:T(8,128)(2,1)S(1)} %get-tuple-element.38), kind=kLoop, calls=%fused_computation.4 | loop fusion | flops 1572864 | bytes 2097152 | tf_op jit(solution)/shard_map/stack | solution.py:208
  79.8 10.0 %gate.1 = (f32[512,4096]{1,0:T(8,128)}, f32[512,128]{1,0:T(8,128)S(1)}) custom-call(f32[512,4096]{1,0:T(8,128)} %intra.1.y_ref, bf16[512,4096]{1,0:T(8,128)(2,1)} %z_ref.1, bf16[512,512]{1,0:T(8,128)(2,1)S(1)} %get-tuple-element.14.c_ref, bf16[4,512,32]{2,1,0:T(8,128)(2,1)S(1)} %copy.56.link_ref, bf16[32,1024]{1,0:T(8,128)(2,1)S(1)} %fusion.22.expand_ref, ...), custom_call_target="tpu_custom_call" | custom-call | tf_op jit(solution)/shard_map/gate/pallas_call | solution.py:344
  89.8 0.1 reduce_sum.9
  89.9 0.1 copy.58
  90.1 1.5 %collective-permute-done.8 = f32[512,1]{1,0:T(8,128)S(1)} collective-permute-done((f32[512,1]{1,0:T(8,128)S(1)}, f32[512,1]{1,0:T(8,128)S(1)}, u32[]{:S(2)}, u32[]{:S(2)}) %collective-permute-start.8) | collective-permute-done | bytes 2080 | tf_op jit(solution)/shard_map/ppermute | solution.py:364
  91.7 6.1 %norm.1 = bf16[512,4096]{1,0:T(8,128)(2,1)} custom-call(f32[512,4096]{1,0:T(8,128)} %get-tuple-element.17.gated_ref, f32[512,1]{1,0:T(8,128)S(1)} %add.162.total_ref, f32[1,4096]{1,0:T(1,128)S(1)} %bitcast.131), custom_call_target="tpu_custom_call" | custom-call | tf_op jit(solution)/shard_map/norm/pallas_call | solution.py:366
  (50 shorter events, 1.0 us)
Async XLA Ops:
  0.0 11.8 %copy-start.3 = (bf16[512,2,512]{2,1,0:T(2,128)(2,1)S(1)}, bf16[512,2,512]{2,1,0:T(2,128)(2,1)}, u32[]{:S(2)}) copy-start(bf16[512,2,512]{2,1,0:T(2,128)(2,1)} %param.14) | copy-start | bytes 3145732
  2.5 10.8 %collective-permute-start = (bf16[8,5248]{1,0:T(8,128)(2,1)S(1)}, bf16[8,5248]{1,0:T(8,128)(2,1)S(1)}, u32[]{:S(2)}, u32[]{:S(2)}) collective-permute-start(bf16[8,5248]{1,0:T(8,128)(2,1)S(1)} %pad_maximum_fusion.6), channel_id=1, source_target_pairs={{0,2},{2,4},{4,6},{6,8},{8,10},{10,12},{12,14},{14,16},{16,18},{18... | collective-permute-start | bytes 251912 | tf_op jit(solution)/shard_map/ppermute | solution.py:235
  11.7 1.8 %copy-start.7 = (s32[512]{0:T(512)S(1)}, s32[512]{0:T(512)}, u32[]{:S(2)}) copy-start(s32[512]{0:T(512)} %param.25) | copy-start | bytes 6148
  14.5 1.5 %copy-start = (bf16[4,4096]{1,0:T(4,128)(2,1)S(1)}, bf16[4,4096]{1,0:T(4,128)(2,1)}, u32[]{:S(2)}) copy-start(bf16[4,4096]{1,0:T(4,128)(2,1)} %wx_ref.1) | copy-start | bytes 98308
  14.6 1.5 %copy-start.1 = (f32[4096]{0:T(1024)S(1)}, f32[4096]{0:T(1024)}, u32[]{:S(2)}) copy-start(f32[4096]{0:T(1024)} %param.19) | copy-start | bytes 49156
  28.4 5.8 %copy-start.8 = (f32[64]{0:T(128)S(1)}, f32[64]{0:T(128)}, u32[]{:S(2)}) copy-start(f32[64]{0:T(128)} %param.23) | copy-start | bytes 772
  30.6 11.1 %collective-permute-start.3 = (bf16[144,1024]{1,0:T(8,128)(2,1)}, bf16[144,1024]{1,0:T(8,128)(2,1)S(1)}, u32[]{:S(2)}, u32[]{:S(2)}) collective-permute-start(bf16[144,1024]{1,0:T(8,128)(2,1)} %get-tuple-element.35), channel_id=1, source_target_pairs={{0,6},{2,4},{4,2},{6,0},{8,14},{10,12},{12,10},{14,8},{16,22},{18,... | collective-permute-start | bytes 884744 | tf_op jit(solution)/shard_map/ppermute | solution.py:188
  33.1 13.4 %collective-permute-start.2 = (bf16[144,1024]{1,0:T(8,128)(2,1)}, bf16[144,1024]{1,0:T(8,128)(2,1)S(1)}, u32[]{:S(2)}, u32[]{:S(2)}) collective-permute-start(bf16[144,1024]{1,0:T(8,128)(2,1)} %get-tuple-element.36), channel_id=1, source_target_pairs={{0,4},{2,6},{4,0},{6,2},{8,12},{10,14},{12,8},{14,10},{16,20},{18,... | collective-permute-start | bytes 884744 | tf_op jit(solution)/shard_map/ppermute | solution.py:188
  33.6 13.0 %collective-permute-start.1 = (bf16[144,1024]{1,0:T(8,128)(2,1)S(1)}, bf16[144,1024]{1,0:T(8,128)(2,1)S(1)}, u32[]{:S(2)}, u32[]{:S(2)}) collective-permute-start(bf16[144,1024]{1,0:T(8,128)(2,1)S(1)} %get-tuple-element.37), channel_id=1, source_target_pairs={{0,2},{2,0},{4,6},{6,4},{8,10},{10,8},{12,14},{14,12},{16,18},{18,... | collective-permute-start | bytes 884744 | tf_op jit(solution)/shard_map/ppermute | solution.py:188
  41.7 4.9 %copy-start.4 = (bf16[144,1024]{1,0:T(8,128)(2,1)}, bf16[144,1024]{1,0:T(8,128)(2,1)S(1)}, u32[]{:S(2)}) copy-start(bf16[144,1024]{1,0:T(8,128)(2,1)S(1)} %collective-permute-done.3) | copy-start | bytes 884740
  46.5 0.7 copy-start.5
  46.6 0.7 copy-start.6
  49.6 13.6 %collective-permute-start.4 = (bf16[128,1024]{1,0:T(8,128)(2,1)}, bf16[128,1024]{1,0:T(8,128)(2,1)S(1)}, u32[]{:S(2)}, u32[]{:S(2)}) collective-permute-start(bf16[128,1024]{1,0:T(8,128)(2,1)} %fusion.6), channel_id=1, source_target_pairs={{0,8},{2,10},{4,12},{6,14},{8,16},{10,18},{12,20},{14,22},{16,24},... | collective-permute-start | bytes 786440 | tf_op jit(solution)/shard_map/ppermute | solution.py:203
  63.8 10.2 %collective-permute-start.7 = (bf16[128,1024]{1,0:T(8,128)(2,1)S(1)}, bf16[128,1024]{1,0:T(8,128)(2,1)S(1)}, u32[]{:S(2)}, u32[]{:S(2)}) collective-permute-start(bf16[128,1024]{1,0:T(8,128)(2,1)S(1)} %get-tuple-element.43), channel_id=1, source_target_pairs={{0,6},{2,4},{4,2},{6,0},{8,14},{10,12},{12,10},{14,8},{16,22},{18,... | collective-permute-start | bytes 786440 | tf_op jit(solution)/shard_map/ppermute | solution.py:188
  65.6 12.7 %collective-permute-start.6 = (bf16[128,1024]{1,0:T(8,128)(2,1)S(1)}, bf16[128,1024]{1,0:T(8,128)(2,1)S(1)}, u32[]{:S(2)}, u32[]{:S(2)}) collective-permute-start(bf16[128,1024]{1,0:T(8,128)(2,1)S(1)} %get-tuple-element.44), channel_id=1, source_target_pairs={{0,4},{2,6},{4,0},{6,2},{8,12},{10,14},{12,8},{14,10},{16,20},{18,... | collective-permute-start | bytes 786440 | tf_op jit(solution)/shard_map/ppermute | solution.py:188
  66.8 11.6 %collective-permute-start.5 = (bf16[128,1024]{1,0:T(8,128)(2,1)S(1)}, bf16[128,1024]{1,0:T(8,128)(2,1)S(1)}, u32[]{:S(2)}, u32[]{:S(2)}) collective-permute-start(bf16[128,1024]{1,0:T(8,128)(2,1)S(1)} %get-tuple-element.45), channel_id=1, source_target_pairs={{0,2},{2,0},{4,6},{6,4},{8,10},{10,8},{12,14},{14,12},{16,18},{18,... | collective-permute-start | bytes 786440 | tf_op jit(solution)/shard_map/ppermute | solution.py:188
  89.8 1.9 %copy-start.2 = (f32[4096]{0:T(1024)S(1)}, f32[4096]{0:T(1024)}, u32[]{:S(2)}) copy-start(f32[4096]{0:T(1024)} %param.24) | copy-start | bytes 49156
  90.1 1.6 %collective-permute-start.8 = (f32[512,1]{1,0:T(8,128)S(1)}, f32[512,1]{1,0:T(8,128)S(1)}, u32[]{:S(2)}, u32[]{:S(2)}) collective-permute-start(f32[512,1]{1,0:T(8,128)S(1)} %copy.58), channel_id=1, source_target_pairs={{0,1},{1,0},{2,3},{3,2},{4,5},{5,4},{6,7},{7,6},{8,9},{9,8},{10,11... | collective-permute-start | bytes 6152 | tf_op jit(solution)/shard_map/ppermute | solution.py:364

commit v3 on v2

--- a/solution.py
+++ b/solution.py
@@ -32,10 +32,18 @@
     return silu(acc).astype(BF16)
 
 
+def selector(depth, width, start):
+    row = lax.broadcasted_iota(jnp.int32, (depth, width), 0)
+    lane = lax.broadcasted_iota(jnp.int32, (depth, width), 1) + start
+    head = jnp.where(row >= depth // 2, row - depth // 2, row)
+    low = head * 64
+    return jnp.where((lane >= low) & (lane < low + 64), 1.0, 0.0).astype(BF16)
+
+
 def local_kernel(
     x_ref, rim_ref, b_ref, c_ref, rimb_ref, rimc_ref, wx_ref, wb_ref, wc_ref,
-    bx_ref, bb_ref, bc_ref, counted_ref, tail_ref, gain_ref, row_gain_ref, expand_ref,
-    xo_ref, bo_ref, co_ref, inc_ref, sum_ref, window, window_b, window_c, weighted, masks,
+    bx_ref, bb_ref, bc_ref, counted_ref, tail_ref, gain_ref, row_gain_ref,
+    xo_ref, bo_ref, co_ref, inc_ref, sum_ref, window, window_b, window_c, weighted, masks, expand,
 ):
     rows, width = x_ref.shape
     blocks = rows // STRETCH
@@ -45,6 +53,7 @@
         for tap in range(3):
             masks[tap] = jnp.broadcast_to(counted_ref[:, tap : tap + 1], (rows, 128))
 
+    expand[...] = selector(*expand.shape, pl.program_id(0) * width)
     window_b[0:RIM] = rimb_ref[...].astype(F32)
     window_c[0:RIM] = rimc_ref[...].astype(F32)
     window_b[RIM:] = b_ref[...].astype(F32)
@@ -69,7 +78,7 @@
             )
             xo_ref[at, lanes] = value
             spread = jnp.dot(
-                tail_ref[0, at, :], expand_ref[:, lanes], preferred_element_type=F32
+                tail_ref[at, :], expand[:, lanes], preferred_element_type=F32
             )
             weighted[at, lanes] = (value.astype(F32) * spread).astype(BF16)
     parts = []
@@ -86,7 +95,8 @@
 
 
 def intra_kernel(
-    x_ref, b_ref, c_ref, col_ref, row_ref, ids_ref, idr_ref, skip_ref, y_ref
+    x_ref, b_ref, c_ref, col_ref, row_ref, ids_ref, idr_ref, skip_ref,
+    link_ref, inc_ref, y_ref, expand,
 ):
     rows, width = x_ref.shape
     blocks = rows // STRETCH
@@ -96,6 +106,7 @@
     t_at = lax.broadcasted_iota(jnp.int32, (STRETCH, STRETCH), 0)
     s_at = lax.broadcasted_iota(jnp.int32, (STRETCH, STRETCH), 1)
     lower = s_at <= t_at
+    expand[...] = selector(*expand.shape, pl.program_id(0) * width)
     for block in range(blocks):
         at = slice(block * STRETCH, (block + 1) * STRETCH)
         scores = lax.dot_general(
@@ -124,15 +135,20 @@
                 lower_sum = low if which == 0 else lower_sum + low
             skip = skip_ref[:, lanes]
             wide = value.astype(F32)
-            y_ref[at.start : at.start + half, lanes] = upper_sum + skip * wide[:half]
-            y_ref[at.start + half : at.stop, lanes] = lower_sum + skip * wide[half:]
-
-
-def gate_kernel(
-    y_ref, z_ref, c_ref, link_ref, expand_ref, enter_ref, inc_ref, row_gain_ref, out_ref, sq_ref
-):
+            base = skip * wide
+            if block == 1:
+                carried = jnp.dot(
+                    c_ref[at], inc_ref[0, :, lanes].astype(BF16), preferred_element_type=F32
+                )
+                link = jnp.dot(link_ref[at], expand[:, lanes], preferred_element_type=F32)
+                base = base + carried * link
+            y_ref[at.start : at.start + half, lanes] = upper_sum + base[:half]
+            y_ref[at.start + half : at.stop, lanes] = lower_sum + base[half:]
+
+
+def gate_kernel(y_ref, z_ref, c_ref, link_ref, enter_ref, out_ref, sq_ref, expand):
     rows, width = y_ref.shape
-    blocks = rows // STRETCH
+    expand[...] = selector(*expand.shape, pl.program_id(0) * width)
 
     @pl.when(pl.program_id(0) == 0)
     def _():
@@ -140,15 +156,10 @@
 
     for tile in range(width // 256):
         lanes = slice(tile * 256, (tile + 1) * 256)
-        state = enter_ref[0, :, lanes]
-        for block in range(blocks):
-            at = slice(block * STRETCH, (block + 1) * STRETCH)
-            if block == 1:
-                state = (
-                    row_gain_ref[0:1, lanes] * state.astype(F32) + inc_ref[0, :, lanes]
-                ).astype(BF16)
-            inter = jnp.dot(c_ref[at], state, preferred_element_type=F32)
-            link = jnp.dot(link_ref[0, at], expand_ref[:, lanes], preferred_element_type=F32)
+        for start in range(0, rows, STRETCH):
+            at = slice(start, start + STRETCH)
+            inter = jnp.dot(c_ref[at], enter_ref[0, :, lanes], preferred_element_type=F32)
+            link = jnp.dot(link_ref[at], expand[:, lanes], preferred_element_type=F32)
             gate = silu(z_ref[at, lanes].astype(F32))
             gated = (y_ref[at, lanes] + inter * link) * gate
             out_ref[at, lanes] = gated
@@ -166,7 +177,7 @@
     return jnp.concatenate([high, (value - high.astype(F32)).astype(BF16)], axis=-1)
 
 
-def exchange(sums, groups):
+def exchange(sums, groups, beside):
     axis = "seq"
     count = lax.axis_size(axis)
     plane = count // 4
@@ -189,7 +200,7 @@
             )
         return jnp.stack(got)
 
-    came = swap(chunks)
+    came, beside = lax.optimization_barrier((swap(chunks), beside))
     run = jnp.zeros((STATE, cut), F32)
     through = jnp.ones((1, cut), F32)
     entering, gains = [], []
@@ -207,7 +218,7 @@
     back = swap(ready)
     final = jnp.stack([pick(back, place ^ owner) for owner in range(plane)])
     final = final.reshape(groups, split, STATE, cut).transpose(0, 2, 1, 3)
-    return final.reshape(groups, STATE, width)
+    return final.reshape(groups, STATE, width), beside
 
 
 def on_device(
@@ -256,8 +267,10 @@
     def by_group(value):
         return value.reshape(rows, groups, per).transpose(1, 0, 2)
 
-    tail_two = split_two(by_group(tail))
-    link_two = split_two(by_group(link))
+    flat = lambda value: split_two(value.reshape(rows, heads))
+    tail_two, link_two = flat(tail), flat(link)
+    reach = jnp.concatenate([jnp.ones_like(gain[:1]), gain[:1]])[:, None]
+    reach_two = flat(link * reach)
     col = by_group(cum)
     shifted = cum - jnp.log2(steps)
     row = shifted.reshape(blocks, STRETCH, groups, per).transpose(2, 0, 3, 1)
@@ -267,11 +280,6 @@
     whole_low = (whole - whole_high.astype(F32)).astype(BF16)
     gain_rows = jnp.stack([whole_high, whole_low]).reshape(2, groups, width).transpose(1, 0, 2)
     gain_rows = jnp.pad(gain_rows, ((0, 0), (0, 14), (0, 0)))
-    expand = (
-        lax.broadcasted_iota(jnp.int32, (2 * per, width), 0) % per
-        == lax.broadcasted_iota(jnp.int32, (2 * per, width), 1) // size
-    ).astype(BF16)
-
     params = pltpu.CompilerParams(vmem_limit_bytes=VMEM)
     wide = lambda n: pl.BlockSpec((n, width), lambda g: (0, g))
     state_b = lambda n: pl.BlockSpec((n, STATE), lambda g: (0, g))
@@ -288,8 +296,7 @@
         in_specs=[
             wide(rows), wide(RIM), state_b(rows), state_c(rows), rim_b, rim_c,
             wide(4), state_b(4), state_c(4), wide(1), state_b(1), state_c(1),
-            full(rows, 3), lead(rows, 2 * per), lead(16, width), wide(blocks),
-            full(2 * per, width),
+            full(rows, 3), full(rows, 2 * heads), lead(16, width), wide(blocks),
         ],
         out_specs=[
             wide(rows), state_b(rows), state_b(rows), lead(STATE, width),
@@ -308,6 +315,7 @@
             pltpu.VMEM((rows + RIM, STATE), F32),
             pltpu.VMEM((rows, width), BF16),
             pltpu.VMEM((3, rows, 128), F32),
+            pltpu.VMEM((2 * heads, width), BF16),
         ],
         compiler_params=params,
         cost_estimate=pl.CostEstimate(
@@ -316,10 +324,8 @@
         name="local",
     )(
         x_proj, rim, bc_flat, bc_flat, rim, rim, conv_x, wbc, wbc, bias_row, bbc, bbc,
-        counted, tail_two, gain_rows, row_gain, expand,
+        counted, tail_two, gain_rows, row_gain,
     )
-
-    enter = exchange(sums, groups)
 
     y = pl.pallas_call(
         intra_kernel,
@@ -327,7 +333,9 @@
         in_specs=[
             wide(rows), state_b(rows), state_b(rows), lead(rows, per),
             lead(blocks, per, STRETCH), full(rows, 1), full(blocks, STRETCH), wide(1),
-        ],
+            full(rows, 2 * heads), lead(STATE, width),
+        ],
+        scratch_shapes=[pltpu.VMEM((2 * heads, width), BF16)],
         out_specs=wide(rows),
         out_shape=jax.ShapeDtypeStruct((rows, inner), F32),
         compiler_params=params,
@@ -338,34 +346,40 @@
         name="intra",
     )(
         x_conv, b_conv, c_conv, col, row, seg_ids.reshape(rows, 1), ids,
-        jnp.repeat(d_skip, size).reshape(1, inner),
+        jnp.repeat(d_skip, size).reshape(1, inner), link_two, inc,
     )
 
+    enter, y = exchange(sums, groups, y)
+
+    narrow = width // 2
+    slab = pl.BlockSpec((rows, narrow), lambda g: (0, g))
     gated, squares = pl.pallas_call(
         gate_kernel,
-        grid=(groups,),
+        grid=(2 * groups,),
         in_specs=[
-            wide(rows), wide(rows), state_b(rows), lead(rows, 2 * per), full(2 * per, width),
-            lead(STATE, width), lead(STATE, width), wide(blocks),
-        ],
-        out_specs=[wide(rows), full(rows, 128)],
+            slab, slab, pl.BlockSpec((rows, STATE), lambda g: (0, g // 2)),
+            full(rows, 2 * heads),
+            pl.BlockSpec((1, STATE, narrow), lambda g: (g // 2, 0, g % 2)),
+        ],
+        out_specs=[slab, full(rows, 128)],
         out_shape=[
             jax.ShapeDtypeStruct((rows, inner), F32),
             jax.ShapeDtypeStruct((rows, 128), F32),
         ],
+        scratch_shapes=[pltpu.VMEM((2 * heads, narrow), BF16)],
         compiler_params=params,
         name="gate",
-    )(y, z_proj, c_conv, link_two, expand, enter, inc, row_gain)
+    )(y, z_proj, c_conv, reach_two, enter)
 
     total = jnp.sum(squares, axis=-1, keepdims=True)
     count = lax.axis_size("tp")
     own = total
     for k in range(1, count):
         total = total + lax.ppermute(own, "tp", [(i, (i + k) % count) for i in range(count)])
-    part = rows // 4
+    part = rows // 8
     return pl.pallas_call(
         functools.partial(norm_kernel, channels=inner * count),
-        grid=(4,),
+        grid=(8,),
         in_specs=[
             pl.BlockSpec((part, inner), lambda r: (r, 0)),
             pl.BlockSpec((part, 1), lambda r: (r, 0)),

time: 98.4 us -> 92.5 us (0.940)
  Pallas kernels: 38.4 us -> 43.4 us
  waiting for transfers between devices: 22.8 us -> 18.3 us
  local copies, waits for them, and re-layouts: 13 us -> 8.78 us
  other arithmetic: 7.37 us -> 4.83 us
    ppermute x6, waiting for transfers between devices: 21.3 us -> 11.3 us  [swap(): lax.ppermute(pick(array, place ^ k), axis, [(i, i ^ k) for i in range(cou...]
    ppermute x1, waiting for transfers between devices: 0.01 us -> 5.49 us  [exchange(): lax.ppermute(run.astype(BF16), axis, [(i, i + plane) for i in range(count...]
    pallas_call x1, Pallas kernels: 6.12 us -> 8.07 us  [on_device(): pl.pallas_call(functools.partial(norm_kernel, channels=inner * count), gr...]
    unnamed x23 -> x21, local copies, waits for them, and re-layouts: 4.09 us -> 2.17 us
    pallas_call x1, Pallas kernels: 9.99 us -> 11.4 us  [on_device(): pl.pallas_call(gate_kernel, grid=(2 * groups,), in_specs=[slab, slab, pl....]
    pallas_call x1, Pallas kernels: 9.92 us -> 11.2 us  [on_device(): pl.pallas_call(intra_kernel, grid=(groups,), in_specs=[wide(rows), state_...]
    concatenate x2 -> x1, local copies, waits for them, and re-layouts: 1.29 us -> 0.01 us  [on_device(): reach = jnp.concatenate([jnp.ones_like(gain[:1]), gain[:1]])[:, None]]
    another operation x2, other arithmetic: 1.42 us -> 0.28 us  [swap(): return jnp.stack(got)]
  transfers between devices with their start and end apart: 9 -> 9, of which waited for: 7 -> 7; matrix products, arithmetic and copies ran while one was open for 8% -> 7% of each run, Pallas kernels for 10% -> 12%
where the time goes in v3:
time: 92.5 us; the launch traced here: 91.7 us
  Pallas kernels  43.4 us (47%)
  waiting for transfers between devices  18.3 us (20%)
  starting transfers between devices  15.5 us (17%)
  local copies, waits for them, and re-layouts  8.78 us (9%)
  other arithmetic  4.83 us (5%)
    pallas_call x1, Pallas kernels, on_device(): pl.pallas_call(local_kernel, grid=(groups,), in_specs=[wide(rows), wide(R...  12.7 us
    pallas_call x1, Pallas kernels, on_device(): pl.pallas_call(gate_kernel, grid=(2 * groups,), in_specs=[slab, slab, pl....  11.4 us
    ppermute x6, waiting for transfers between devices, swap(): lax.ppermute(pick(array, place ^ k), axis, [(i, i ^ k) for i in range(cou...  11.3 us
    pallas_call x1, Pallas kernels, on_device(): pl.pallas_call(intra_kernel, grid=(groups,), in_specs=[wide(rows), state_...  11.2 us
    pallas_call x1, Pallas kernels, on_device(): pl.pallas_call(functools.partial(norm_kernel, channels=inner * count), gr...  8.07 us
    ppermute x6, starting transfers between devices, swap(): lax.ppermute(pick(array, place ^ k), axis, [(i, i ^ k) for i in range(cou...  7.11 us
    ppermute x1, waiting for transfers between devices, exchange(): lax.ppermute(run.astype(BF16), axis, [(i, i + plane) for i in range(count...  5.49 us
    ppermute x1, starting transfers between devices, on_device(): rim = lax.ppermute(jnp.concatenate(ends, axis=1), 'seq', route)  4.84 us
  transfers between devices with their start and end apart: 9, of which 7 were waited for; matrix products, arithmetic and copies ran while one was open for 7% of the time, Pallas kernels for 12%

profile of v3, /device:TPU:0, one launch (start us, length us, event | category | flops | bytes accessed | tf_op | source)
XLA Modules:
  0.0 91.7 jit_solution(704249054261147599)
XLA Ops:
  0.0 0.8 convert.12
  0.8 0.1 slice.95
  0.8 0.7 slice_bitcast_fusion
  1.6 0.8 slice.93
  2.5 4.8 %collective-permute-start = (bf16[8,5248]{1,0:T(8,128)(2,1)S(1)}, bf16[8,5248]{1,0:T(8,128)(2,1)S(1)}, u32[]{:S(2)}, u32[]{:S(2)}) collective-permute-start(bf16[8,5248]{1,0:T(8,128)(2,1)S(1)} %pad_maximum_fusion.7), channel_id=1, source_target_pairs={{0,2},{2,4},{4,6},{6,8},{8,10},{10,12},{12,14},{14,16},{16,18},{18... | collective-permute-start | bytes 251912 | tf_op jit(solution)/shard_map/ppermute | solution.py:246
  7.4 0.7 reshape.331.idr_ref
  8.1 0.7 negate_multiply_fusion
  8.7 1.1 %broadcast_multiply_fusion.1 = (f32[512,64]{0,1:T(8,128)S(1)}, f32[512,64]{0,1:T(8,128)S(1)}) fusion(f32[64]{0:T(128)S(1)} %negate_multiply_fusion, f32[512,64]{0,1:T(8,128)} %param.16, f32[64]{0:T(128)} %param.21), kind=kLoop, calls=%fused_computation.63 | loop fusion | flops 262144 | bytes 393728 | tf_op jit(solution)/shard_map/mul | solution.py:257
  9.8 0.4 convolution_bitcast_fusion
  10.2 0.2 slice_reduce_fusion
  10.4 0.1 copy.50
  10.6 0.1 reshape_reshape.3.skip_ref
  10.7 0.1 reshape.334
  10.8 0.1 copy.55.ids_ref
  11.0 1.3 %copy.51 = f32[512,4,16]{2,0,1:T(8,128)} copy(f32[512,4,16]{0,2,1:T(8,128)S(1)} %reshape.334) | data formatting | bytes 262144 | tf_op jit(solution)/shard_map/reshape | solution.py:268
  12.3 1.2 %copy.62 = bf16[64,8,2,512]{3,1,2,0:T(8,128)(2,1)} copy(bf16[64,8,2,512]{3,2,1,0:T(2,128)(2,1)S(1)} %bitcast.136) | data formatting | bytes 2097152
  13.5 0.2 slice_reduce_fusion.1
  13.7 0.1 convert_reduce_fusion
  13.8 0.1 pad_add_fusion
  13.9 0.1 slice.103
  14.0 0.1 slice_compare_fusion.2
  14.2 0.1 copy.49.counted_ref
  14.4 0.1 mul.158
  14.5 0.1 broadcast_in_dim.38
  14.6 0.1 mul.159
  14.7 0.1 broadcast_in_dim.39
  14.8 0.1 reshape.333.row_gain_ref
  14.9 0.1 broadcast_multiply_fusion
  15.1 0.1 copy.54
  15.3 0.1 copy.48
  15.5 0.1 pad_maximum_fusion.4.tail_ref
  15.6 0.2 copy-done
  15.8 12.7 %local.1 = (bf16[512,4096]{1,0:T(8,128)(2,1)}, bf16[512,512]{1,0:T(8,128)(2,1)S(1)}, bf16[512,512]{1,0:T(8,128)(2,1)S(1)}, f32[4,128,1024]{2,1,0:T(8,128)}, bf16[4,144,1024]{2,1,0:T(8,128)(2,1)}) custom-call(bf16[512,4096]{1,0:T(8,128)(2,1)} %x_ref.1, bf16[8,5248]{1,0:T(8,128)(2,1)S(1)} %collective-permute-done.rim_ref.rimb_ref.rimc_ref, ...), custom_call_target="tpu_custom_call" | custom-call | flops 1073741824 | bytes 31457280 | tf_op jit(solution)/shard_map/local/pallas_call | solution.py:293
  28.6 1.3 %constant_dynamic-slice_fusion.13 = (bf16[1,144,1024]{2,1,0:T(8,128)(2,1)S(1)}, bf16[144,1024]{1,0:T(8,128)(2,1)S(1)}, bf16[144,1024]{1,0:T(8,128)(2,1)S(1)}, bf16[144,1024]{1,0:T(8,128)(2,1)S(1)}) fusion(bf16[4,144,1024]{2,1,0:T(8,128)(2,1)} %get-tuple-element.14, s32[]{:T(128)S(6)} %select_n.44, s32[]{:T(128)S(6)} %select_n.47, s32[]{:T(128)S(6)} %select_n.46, ...), kind=kLoop, calls=%fused_computation.81 | loop fusion | bytes 2359312 | tf_op jit(solution)/shard_map/jit(dynamic_index_in_dim)/dynamic_slice | solution.py:193
  29.9 2.5 %collective-permute-start.3 = (bf16[144,1024]{1,0:T(8,128)(2,1)S(1)}, bf16[144,1024]{1,0:T(8,128)(2,1)S(1)}, u32[]{:S(2)}, u32[]{:S(2)}) collective-permute-start(bf16[144,1024]{1,0:T(8,128)(2,1)S(1)} %get-tuple-element.43), channel_id=1, source_target_pairs={{0,6},{2,4},{4,2},{6,0},{8,14},{10,12},{12,10},{14,8},{16,22},{18,... | collective-permute-start | bytes 884744 | tf_op jit(solution)/shard_map/ppermute | solution.py:199
  32.4 0.5 collective-permute-start.2
  32.9 0.5 collective-permute-start.1
  33.4 0.1 pad_maximum_fusion.5.link_ref
  33.6 11.2 %intra.1.y_ref = f32[512,4096]{1,0:T(8,128)} custom-call(bf16[512,4096]{1,0:T(8,128)(2,1)} %get-tuple-element.15.x_ref, bf16[512,512]{1,0:T(8,128)(2,1)S(1)} %get-tuple-element.16.b_ref, bf16[512,512]{1,0:T(8,128)(2,1)S(1)} %get-tuple-element.17.c_ref, f32[4,512,16]{2,1,0:T(8,128)} %bitcast.137, f32[4,2,16,256]{3,2,1,0:T(8,128)S(1)} %bitcast.127, ...), custom_call_target="tpu_custom_call" | custom-call | flops 21474836480 | bytes 104857600 | tf_op jit(solution)/shard_map/intra/pallas_call | solution.py:330
  44.8 0.9 collective-permute-done.2
  45.6 0.1 collective-permute-done.1
  45.7 0.1 pad_maximum_fusion
  46.0 0.2 fusion.6
  46.2 3.5 %collective-permute-start.4 = (bf16[128,1024]{1,0:T(8,128)(2,1)S(1)}, bf16[128,1024]{1,0:T(8,128)(2,1)S(1)}, u32[]{:S(2)}, u32[]{:S(2)}) collective-permute-start(bf16[128,1024]{1,0:T(8,128)(2,1)S(1)} %fusion.6), channel_id=1, source_target_pairs={{0,8},{2,10},{4,12},{6,14},{8,16},{10,18},{12,20},{14,22},{16,24},... | collective-permute-start | bytes 786440 | tf_op jit(solution)/shard_map/ppermute | solution.py:214
  49.7 0.1 copy.56
  49.8 5.5 %collective-permute-done.4 = bf16[128,1024]{1,0:T(8,128)(2,1)S(1)} collective-permute-done((bf16[128,1024]{1,0:T(8,128)(2,1)S(1)}, bf16[128,1024]{1,0:T(8,128)(2,1)S(1)}, u32[]{:S(2)}, u32[]{:S(2)}) %collective-permute-start.4) | collective-permute-done | bytes 262176 | tf_op jit(solution)/shard_map/ppermute | solution.py:214
  55.3 0.3 fusion.9
  55.6 0.1 pad_maximum_fusion.1
  55.8 0.1 constant_dynamic-slice_fusion.12
  55.8 1.0 %collective-permute-start.7 = (bf16[128,1024]{1,0:T(8,128)(2,1)S(1)}, bf16[128,1024]{1,0:T(8,128)(2,1)S(1)}, u32[]{:S(2)}, u32[]{:S(2)}) collective-permute-start(bf16[128,1024]{1,0:T(8,128)(2,1)S(1)} %get-tuple-element.51), channel_id=1, source_target_pairs={{0,6},{2,4},{4,2},{6,0},{8,14},{10,12},{12,10},{14,8},{16,22},{18,... | collective-permute-start | bytes 786440 | tf_op jit(solution)/shard_map/ppermute | solution.py:199
  56.9 2.0 %collective-permute-start.6 = (bf16[128,1024]{1,0:T(8,128)(2,1)S(1)}, bf16[128,1024]{1,0:T(8,128)(2,1)S(1)}, u32[]{:S(2)}, u32[]{:S(2)}) collective-permute-start(bf16[128,1024]{1,0:T(8,128)(2,1)S(1)} %get-tuple-element.52), channel_id=1, source_target_pairs={{0,4},{2,6},{4,0},{6,2},{8,12},{10,14},{12,8},{14,10},{16,20},{18,... | collective-permute-start | bytes 786440 | tf_op jit(solution)/shard_map/ppermute | solution.py:199
  58.9 0.5 collective-permute-start.5
  59.4 0.1 pad_maximum_fusion.6.link_ref
  59.6 6.5 %collective-permute-done.7 = bf16[128,1024]{1,0:T(8,128)(2,1)S(1)} collective-permute-done((bf16[128,1024]{1,0:T(8,128)(2,1)S(1)}, bf16[128,1024]{1,0:T(8,128)(2,1)S(1)}, u32[]{:S(2)}, u32[]{:S(2)}) %collective-permute-start.7) | collective-permute-done | bytes 262176 | tf_op jit(solution)/shard_map/ppermute | solution.py:199
  66.1 3.6 %collective-permute-done.6 = bf16[128,1024]{1,0:T(8,128)(2,1)S(1)} collective-permute-done((bf16[128,1024]{1,0:T(8,128)(2,1)S(1)}, bf16[128,1024]{1,0:T(8,128)(2,1)S(1)}, u32[]{:S(2)}, u32[]{:S(2)}) %collective-permute-start.6) | collective-permute-done | bytes 262176 | tf_op jit(solution)/shard_map/ppermute | solution.py:199
  69.7 0.2 collective-permute-done.5
  69.9 0.1 pad_maximum_fusion.2
  70.0 0.1 constant_dynamic-slice_fusion.11
  70.1 0.1 pad_maximum_fusion.3.enter_ref
  70.3 11.4 %gate.1 = (f32[512,4096]{1,0:T(8,128)}, f32[512,128]{1,0:T(8,128)S(1)}) custom-call(f32[512,4096]{1,0:T(8,128)} %intra.1.y_ref, bf16[512,4096]{1,0:T(8,128)(2,1)} %z_ref.1, bf16[512,512]{1,0:T(8,128)(2,1)S(1)} %get-tuple-element.17.c_ref, bf16[512,128]{1,0:T(8,128)(2,1)S(1)} %pad_maximum_fusion.6.link_ref, bf16[4,128,1024]{2,1,0:T(8,128)(2,1)S(1)} %pad_maximum_fusion.3.enter_ref), custom_call_target="tpu_custom_call" | custom-call | tf_op jit(solution)/shard_map/gate/pallas_call | solution.py:356
  81.6 0.1 reduce_sum.9
  81.8 0.1 copy.58
  82.0 1.5 %collective-permute-done.8 = f32[512,1]{1,0:T(8,128)S(1)} collective-permute-done((f32[512,1]{1,0:T(8,128)S(1)}, f32[512,1]{1,0:T(8,128)S(1)}, u32[]{:S(2)}, u32[]{:S(2)}) %collective-permute-start.8) | collective-permute-done | bytes 2080 | tf_op jit(solution)/shard_map/ppermute | solution.py:378
  83.6 8.1 %norm.1 = bf16[512,4096]{1,0:T(8,128)(2,1)} custom-call(f32[512,4096]{1,0:T(8,128)} %get-tuple-element.21.gated_ref, f32[512,1]{1,0:T(8,128)S(1)} %add.152.total_ref, f32[1,4096]{1,0:T(1,128)S(1)} %bitcast.133), custom_call_target="tpu_custom_call" | custom-call | tf_op jit(solution)/shard_map/norm/pallas_call | solution.py:380
  (43 shorter events, 0.8 us)
Async XLA Ops:
  0.0 10.8 %copy-start.4 = (s32[512]{0:T(512)S(1)}, s32[512]{0:T(512)}, u32[]{:S(2)}) copy-start(s32[512]{0:T(512)} %param.25) | copy-start | bytes 6148
  0.0 10.5 %copy-start.6 = (f32[2,512]{1,0:T(2,128)S(1)}, f32[2,512]{1,0:T(2,128)}, u32[]{:S(2)}) copy-start(f32[2,512]{1,0:T(2,128)} %param.20) | copy-start | bytes 12292
  0.0 10.5 %copy-start.5 = (bf16[4,2,512]{2,1,0:T(2,128)(2,1)S(1)}, bf16[4,2,512]{2,1,0:T(2,128)(2,1)}, u32[]{:S(2)}) copy-start(bf16[4,2,512]{2,1,0:T(2,128)(2,1)} %param.18) | copy-start | bytes 24580
  0.0 10.5 %copy-start.7 = (f32[64]{0:T(128)S(1)}, f32[64]{0:T(128)}, u32[]{:S(2)}) copy-start(f32[64]{0:T(128)} %param.23) | copy-start | bytes 772
  2.5 11.2 %collective-permute-start = (bf16[8,5248]{1,0:T(8,128)(2,1)S(1)}, bf16[8,5248]{1,0:T(8,128)(2,1)S(1)}, u32[]{:S(2)}, u32[]{:S(2)}) collective-permute-start(bf16[8,5248]{1,0:T(8,128)(2,1)S(1)} %pad_maximum_fusion.7), channel_id=1, source_target_pairs={{0,2},{2,4},{4,6},{6,8},{8,10},{10,12},{12,14},{14,16},{16,18},{18... | collective-permute-start | bytes 251912 | tf_op jit(solution)/shard_map/ppermute | solution.py:246
  9.8 2.5 %copy-start.3 = (bf16[512,2,512]{2,1,0:T(2,128)(2,1)S(1)}, bf16[512,2,512]{2,1,0:T(2,128)(2,1)}, u32[]{:S(2)}) copy-start(bf16[512,2,512]{2,1,0:T(2,128)(2,1)} %param.14) | copy-start | bytes 3145732
  15.1 0.8 copy-start
  15.1 0.8 copy-start.1
  29.9 14.9 %collective-permute-start.3 = (bf16[144,1024]{1,0:T(8,128)(2,1)S(1)}, bf16[144,1024]{1,0:T(8,128)(2,1)S(1)}, u32[]{:S(2)}, u32[]{:S(2)}) collective-permute-start(bf16[144,1024]{1,0:T(8,128)(2,1)S(1)} %get-tuple-element.43), channel_id=1, source_target_pairs={{0,6},{2,4},{4,2},{6,0},{8,14},{10,12},{12,10},{14,8},{16,22},{18,... | collective-permute-start | bytes 884744 | tf_op jit(solution)/shard_map/ppermute | solution.py:199
  32.4 13.2 %collective-permute-start.2 = (bf16[144,1024]{1,0:T(8,128)(2,1)S(1)}, bf16[144,1024]{1,0:T(8,128)(2,1)S(1)}, u32[]{:S(2)}, u32[]{:S(2)}) collective-permute-start(bf16[144,1024]{1,0:T(8,128)(2,1)S(1)} %get-tuple-element.44), channel_id=1, source_target_pairs={{0,4},{2,6},{4,0},{6,2},{8,12},{10,14},{12,8},{14,10},{16,20},{18,... | collective-permute-start | bytes 884744 | tf_op jit(solution)/shard_map/ppermute | solution.py:199
  32.9 12.8 %collective-permute-start.1 = (bf16[144,1024]{1,0:T(8,128)(2,1)S(1)}, bf16[144,1024]{1,0:T(8,128)(2,1)S(1)}, u32[]{:S(2)}, u32[]{:S(2)}) collective-permute-start(bf16[144,1024]{1,0:T(8,128)(2,1)S(1)} %get-tuple-element.45), channel_id=1, source_target_pairs={{0,2},{2,0},{4,6},{6,4},{8,10},{10,8},{12,14},{14,12},{16,18},{18,... | collective-permute-start | bytes 884744 | tf_op jit(solution)/shard_map/ppermute | solution.py:199
  46.2 9.1 %collective-permute-start.4 = (bf16[128,1024]{1,0:T(8,128)(2,1)S(1)}, bf16[128,1024]{1,0:T(8,128)(2,1)S(1)}, u32[]{:S(2)}, u32[]{:S(2)}) collective-permute-start(bf16[128,1024]{1,0:T(8,128)(2,1)S(1)} %fusion.6), channel_id=1, source_target_pairs={{0,8},{2,10},{4,12},{6,14},{8,16},{10,18},{12,20},{14,22},{16,24},... | collective-permute-start | bytes 786440 | tf_op jit(solution)/shard_map/ppermute | solution.py:214
  55.8 10.2 %collective-permute-start.7 = (bf16[128,1024]{1,0:T(8,128)(2,1)S(1)}, bf16[128,1024]{1,0:T(8,128)(2,1)S(1)}, u32[]{:S(2)}, u32[]{:S(2)}) collective-permute-start(bf16[128,1024]{1,0:T(8,128)(2,1)S(1)} %get-tuple-element.51), channel_id=1, source_target_pairs={{0,6},{2,4},{4,2},{6,0},{8,14},{10,12},{12,10},{14,8},{16,22},{18,... | collective-permute-start | bytes 786440 | tf_op jit(solution)/shard_map/ppermute | solution.py:199
  56.9 12.8 %collective-permute-start.6 = (bf16[128,1024]{1,0:T(8,128)(2,1)S(1)}, bf16[128,1024]{1,0:T(8,128)(2,1)S(1)}, u32[]{:S(2)}, u32[]{:S(2)}) collective-permute-start(bf16[128,1024]{1,0:T(8,128)(2,1)S(1)} %get-tuple-element.52), channel_id=1, source_target_pairs={{0,4},{2,6},{4,0},{6,2},{8,12},{10,14},{12,8},{14,10},{16,20},{18,... | collective-permute-start | bytes 786440 | tf_op jit(solution)/shard_map/ppermute | solution.py:199
  58.9 11.0 %collective-permute-start.5 = (bf16[128,1024]{1,0:T(8,128)(2,1)S(1)}, bf16[128,1024]{1,0:T(8,128)(2,1)S(1)}, u32[]{:S(2)}, u32[]{:S(2)}) collective-permute-start(bf16[128,1024]{1,0:T(8,128)(2,1)S(1)} %get-tuple-element.53), channel_id=1, source_target_pairs={{0,2},{2,0},{4,6},{6,4},{8,10},{10,8},{12,14},{14,12},{16,18},{18,... | collective-permute-start | bytes 786440 | tf_op jit(solution)/shard_map/ppermute | solution.py:199
  81.6 1.9 %copy-start.2 = (f32[4096]{0:T(1024)S(1)}, f32[4096]{0:T(1024)}, u32[]{:S(2)}) copy-start(f32[4096]{0:T(1024)} %param.24) | copy-start | bytes 49156
  81.9 1.6 %collective-permute-start.8 = (f32[512,1]{1,0:T(8,128)S(1)}, f32[512,1]{1,0:T(8,128)S(1)}, u32[]{:S(2)}, u32[]{:S(2)}) collective-permute-start(f32[512,1]{1,0:T(8,128)S(1)} %copy.58), channel_id=1, source_target_pairs={{0,1},{1,0},{2,3},{3,2},{4,5},{5,4},{6,7},{7,6},{8,9},{9,8},{10,11... | collective-permute-start | bytes 6152 | tf_op jit(solution)/shard_map/ppermute | solution.py:378

commit v4 on v3

--- a/solution.py
+++ b/solution.py
@@ -168,7 +168,9 @@
 
 
 def norm_kernel(gated_ref, total_ref, gain_ref, out_ref, *, channels):
-    scale = lax.rsqrt(total_ref[...] / channels + 1e-05)
+    part = out_ref.shape[0]
+    total = total_ref[pl.ds(pl.multiple_of(pl.program_id(0) * part, part), part), :]
+    scale = lax.rsqrt(total / channels + 1e-05)
     out_ref[...] = (gated_ref[...] * scale * gain_ref[...]).astype(BF16)
 
 
@@ -351,22 +353,18 @@
 
     enter, y = exchange(sums, groups, y)
 
-    narrow = width // 2
-    slab = pl.BlockSpec((rows, narrow), lambda g: (0, g))
     gated, squares = pl.pallas_call(
         gate_kernel,
-        grid=(2 * groups,),
+        grid=(groups,),
         in_specs=[
-            slab, slab, pl.BlockSpec((rows, STATE), lambda g: (0, g // 2)),
-            full(rows, 2 * heads),
-            pl.BlockSpec((1, STATE, narrow), lambda g: (g // 2, 0, g % 2)),
-        ],
-        out_specs=[slab, full(rows, 128)],
+            wide(rows), wide(rows), state_b(rows), full(rows, 2 * heads), lead(STATE, width),
+        ],
+        out_specs=[wide(rows), full(rows, 128)],
         out_shape=[
             jax.ShapeDtypeStruct((rows, inner), F32),
             jax.ShapeDtypeStruct((rows, 128), F32),
         ],
-        scratch_shapes=[pltpu.VMEM((2 * heads, narrow), BF16)],
+        scratch_shapes=[pltpu.VMEM((2 * heads, width), BF16)],
         compiler_params=params,
         name="gate",
     )(y, z_proj, c_conv, reach_two, enter)
@@ -376,13 +374,13 @@
     own = total
     for k in range(1, count):
         total = total + lax.ppermute(own, "tp", [(i, (i + k) % count) for i in range(count)])
-    part = rows // 8
+    part = rows // 4
     return pl.pallas_call(
         functools.partial(norm_kernel, channels=inner * count),
-        grid=(8,),
+        grid=(4,),
         in_specs=[
             pl.BlockSpec((part, inner), lambda r: (r, 0)),
-            pl.BlockSpec((part, 1), lambda r: (r, 0)),
+            full(rows, 1),
             full(1, inner),
         ],
         out_specs=pl.BlockSpec((part, inner), lambda r: (r, 0)),

time: 92.5 us -> 88.4 us (0.956)
  Pallas kernels: 43.4 us -> 39.6 us
    pallas_call x1, Pallas kernels: 8.07 us -> 6.12 us  [on_device(): pl.pallas_call(functools.partial(norm_kernel, channels=inner * count), gr...]
    pallas_call x1, Pallas kernels: 11.4 us -> 9.51 us  [on_device(): pl.pallas_call(gate_kernel, grid=(groups,), in_specs=[wide(rows), wide(ro...]
  transfers between devices with their start and end apart: 9 -> 9, of which waited for: 7 -> 7; matrix products, arithmetic and copies ran while one was open for 7% -> 7% of each run, Pallas kernels for 12% -> 13%
where the time goes in v4:
time: 88.4 us; the launch traced here: 87.9 us
  Pallas kernels  39.6 us (45%)
  waiting for transfers between devices  18.3 us (21%)
  starting transfers between devices  15.5 us (18%)
  local copies, waits for them, and re-layouts  8.78 us (10%)
  other arithmetic  4.83 us (5%)
    pallas_call x1, Pallas kernels, on_device(): pl.pallas_call(local_kernel, grid=(groups,), in_specs=[wide(rows), wide(R...  12.7 us
    ppermute x6, waiting for transfers between devices, swap(): lax.ppermute(pick(array, place ^ k), axis, [(i, i ^ k) for i in range(cou...  11.3 us
    pallas_call x1, Pallas kernels, on_device(): pl.pallas_call(intra_kernel, grid=(groups,), in_specs=[wide(rows), state_...  11.2 us
    pallas_call x1, Pallas kernels, on_device(): pl.pallas_call(gate_kernel, grid=(groups,), in_specs=[wide(rows), wide(ro...  9.51 us
    ppermute x6, starting transfers between devices, swap(): lax.ppermute(pick(array, place ^ k), axis, [(i, i ^ k) for i in range(cou...  7.11 us
    pallas_call x1, Pallas kernels, on_device(): pl.pallas_call(functools.partial(norm_kernel, channels=inner * count), gr...  6.12 us
    ppermute x1, waiting for transfers between devices, exchange(): lax.ppermute(run.astype(BF16), axis, [(i, i + plane) for i in range(count...  5.49 us
    ppermute x1, starting transfers between devices, on_device(): rim = lax.ppermute(jnp.concatenate(ends, axis=1), 'seq', route)  4.84 us
  transfers between devices with their start and end apart: 9, of which 7 were waited for; matrix products, arithmetic and copies ran while one was open for 7% of the time, Pallas kernels for 13%

profile of v4, /device:TPU:0, one launch (start us, length us, event | category | flops | bytes accessed | tf_op | source)
XLA Modules:
  0.0 87.9 jit_solution(16921737486987982986)
XLA Ops:
  0.0 0.8 convert.12
  0.8 0.1 slice.95
  0.8 0.7 slice_bitcast_fusion
  1.6 0.8 slice.93
  2.5 4.8 %collective-permute-start = (bf16[8,5248]{1,0:T(8,128)(2,1)S(1)}, bf16[8,5248]{1,0:T(8,128)(2,1)S(1)}, u32[]{:S(2)}, u32[]{:S(2)}) collective-permute-start(bf16[8,5248]{1,0:T(8,128)(2,1)S(1)} %pad_maximum_fusion.7), channel_id=1, source_target_pairs={{0,2},{2,4},{4,6},{6,8},{8,10},{10,12},{12,14},{14,16},{16,18},{18... | collective-permute-start | bytes 251912 | tf_op jit(solution)/shard_map/ppermute | solution.py:248
  7.4 0.7 reshape.331.idr_ref
  8.1 0.7 negate_multiply_fusion
  8.7 1.1 %broadcast_multiply_fusion.1 = (f32[512,64]{0,1:T(8,128)S(1)}, f32[512,64]{0,1:T(8,128)S(1)}) fusion(f32[64]{0:T(128)S(1)} %negate_multiply_fusion, f32[512,64]{0,1:T(8,128)} %param.16, f32[64]{0:T(128)} %param.21), kind=kLoop, calls=%fused_computation.63 | loop fusion | flops 262144 | bytes 393728 | tf_op jit(solution)/shard_map/mul | solution.py:259
  9.8 0.4 convolution_bitcast_fusion
  10.2 0.2 slice_reduce_fusion
  10.4 0.1 copy.50
  10.6 0.1 reshape_reshape.3.skip_ref
  10.7 0.1 reshape.334
  10.8 0.1 copy.55.ids_ref
  11.0 1.3 %copy.51 = f32[512,4,16]{2,0,1:T(8,128)} copy(f32[512,4,16]{0,2,1:T(8,128)S(1)} %reshape.334) | data formatting | bytes 262144 | tf_op jit(solution)/shard_map/reshape | solution.py:270
  12.3 1.2 %copy.62 = bf16[64,8,2,512]{3,1,2,0:T(8,128)(2,1)} copy(bf16[64,8,2,512]{3,2,1,0:T(2,128)(2,1)S(1)} %bitcast.136) | data formatting | bytes 2097152
  13.5 0.2 slice_reduce_fusion.1
  13.7 0.1 convert_reduce_fusion
  13.8 0.1 pad_add_fusion
  13.9 0.1 slice.103
  14.0 0.1 slice_compare_fusion.2
  14.2 0.1 copy.49.counted_ref
  14.4 0.1 mul.158
  14.5 0.1 broadcast_in_dim.38
  14.6 0.1 mul.159
  14.7 0.1 broadcast_in_dim.39
  14.8 0.1 reshape.333.row_gain_ref
  14.9 0.1 broadcast_multiply_fusion
  15.1 0.1 copy.54
  15.3 0.1 copy.48
  15.5 0.1 pad_maximum_fusion.4.tail_ref
  15.6 0.2 copy-done
  15.8 12.7 %local.1 = (bf16[512,4096]{1,0:T(8,128)(2,1)}, bf16[512,512]{1,0:T(8,128)(2,1)S(1)}, bf16[512,512]{1,0:T(8,128)(2,1)S(1)}, f32[4,128,1024]{2,1,0:T(8,128)}, bf16[4,144,1024]{2,1,0:T(8,128)(2,1)}) custom-call(bf16[512,4096]{1,0:T(8,128)(2,1)} %x_ref.1, bf16[8,5248]{1,0:T(8,128)(2,1)S(1)} %collective-permute-done.rim_ref.rimb_ref.rimc_ref, ...), custom_call_target="tpu_custom_call" | custom-call | flops 1073741824 | bytes 31457280 | tf_op jit(solution)/shard_map/local/pallas_call | solution.py:295
  28.6 1.3 %constant_dynamic-slice_fusion.13 = (bf16[1,144,1024]{2,1,0:T(8,128)(2,1)S(1)}, bf16[144,1024]{1,0:T(8,128)(2,1)S(1)}, bf16[144,1024]{1,0:T(8,128)(2,1)S(1)}, bf16[144,1024]{1,0:T(8,128)(2,1)S(1)}) fusion(bf16[4,144,1024]{2,1,0:T(8,128)(2,1)} %get-tuple-element.14, s32[]{:T(128)S(6)} %select_n.44, s32[]{:T(128)S(6)} %select_n.47, s32[]{:T(128)S(6)} %select_n.46, ...), kind=kLoop, calls=%fused_computation.81 | loop fusion | bytes 2359312 | tf_op jit(solution)/shard_map/jit(dynamic_index_in_dim)/dynamic_slice | solution.py:195
  29.9 2.5 %collective-permute-start.3 = (bf16[144,1024]{1,0:T(8,128)(2,1)S(1)}, bf16[144,1024]{1,0:T(8,128)(2,1)S(1)}, u32[]{:S(2)}, u32[]{:S(2)}) collective-permute-start(bf16[144,1024]{1,0:T(8,128)(2,1)S(1)} %get-tuple-element.43), channel_id=1, source_target_pairs={{0,6},{2,4},{4,2},{6,0},{8,14},{10,12},{12,10},{14,8},{16,22},{18,... | collective-permute-start | bytes 884744 | tf_op jit(solution)/shard_map/ppermute | solution.py:201
  32.4 0.5 collective-permute-start.2
  32.9 0.5 collective-permute-start.1
  33.4 0.1 pad_maximum_fusion.5.link_ref
  33.6 11.2 %intra.1.y_ref = f32[512,4096]{1,0:T(8,128)} custom-call(bf16[512,4096]{1,0:T(8,128)(2,1)} %get-tuple-element.15.x_ref, bf16[512,512]{1,0:T(8,128)(2,1)S(1)} %get-tuple-element.16.b_ref, bf16[512,512]{1,0:T(8,128)(2,1)S(1)} %get-tuple-element.17.c_ref, f32[4,512,16]{2,1,0:T(8,128)} %bitcast.137, f32[4,2,16,256]{3,2,1,0:T(8,128)S(1)} %bitcast.127, ...), custom_call_target="tpu_custom_call" | custom-call | flops 21474836480 | bytes 104857600 | tf_op jit(solution)/shard_map/intra/pallas_call | solution.py:332
  44.8 0.9 collective-permute-done.2
  45.6 0.1 collective-permute-done.1
  45.7 0.1 pad_maximum_fusion
  46.0 0.2 fusion.6
  46.2 3.5 %collective-permute-start.4 = (bf16[128,1024]{1,0:T(8,128)(2,1)S(1)}, bf16[128,1024]{1,0:T(8,128)(2,1)S(1)}, u32[]{:S(2)}, u32[]{:S(2)}) collective-permute-start(bf16[128,1024]{1,0:T(8,128)(2,1)S(1)} %fusion.6), channel_id=1, source_target_pairs={{0,8},{2,10},{4,12},{6,14},{8,16},{10,18},{12,20},{14,22},{16,24},... | collective-permute-start | bytes 786440 | tf_op jit(solution)/shard_map/ppermute | solution.py:216
  49.7 0.1 copy.56
  49.8 5.5 %collective-permute-done.4 = bf16[128,1024]{1,0:T(8,128)(2,1)S(1)} collective-permute-done((bf16[128,1024]{1,0:T(8,128)(2,1)S(1)}, bf16[128,1024]{1,0:T(8,128)(2,1)S(1)}, u32[]{:S(2)}, u32[]{:S(2)}) %collective-permute-start.4) | collective-permute-done | bytes 262176 | tf_op jit(solution)/shard_map/ppermute | solution.py:216
  55.3 0.3 fusion.9
  55.6 0.1 pad_maximum_fusion.1
  55.8 0.1 constant_dynamic-slice_fusion.12
  55.8 1.0 %collective-permute-start.7 = (bf16[128,1024]{1,0:T(8,128)(2,1)S(1)}, bf16[128,1024]{1,0:T(8,128)(2,1)S(1)}, u32[]{:S(2)}, u32[]{:S(2)}) collective-permute-start(bf16[128,1024]{1,0:T(8,128)(2,1)S(1)} %get-tuple-element.51), channel_id=1, source_target_pairs={{0,6},{2,4},{4,2},{6,0},{8,14},{10,12},{12,10},{14,8},{16,22},{18,... | collective-permute-start | bytes 786440 | tf_op jit(solution)/shard_map/ppermute | solution.py:201
  56.9 2.0 %collective-permute-start.6 = (bf16[128,1024]{1,0:T(8,128)(2,1)S(1)}, bf16[128,1024]{1,0:T(8,128)(2,1)S(1)}, u32[]{:S(2)}, u32[]{:S(2)}) collective-permute-start(bf16[128,1024]{1,0:T(8,128)(2,1)S(1)} %get-tuple-element.52), channel_id=1, source_target_pairs={{0,4},{2,6},{4,0},{6,2},{8,12},{10,14},{12,8},{14,10},{16,20},{18,... | collective-permute-start | bytes 786440 | tf_op jit(solution)/shard_map/ppermute | solution.py:201
  58.9 0.5 collective-permute-start.5
  59.4 0.1 pad_maximum_fusion.6.link_ref
  59.6 6.5 %collective-permute-done.7 = bf16[128,1024]{1,0:T(8,128)(2,1)S(1)} collective-permute-done((bf16[128,1024]{1,0:T(8,128)(2,1)S(1)}, bf16[128,1024]{1,0:T(8,128)(2,1)S(1)}, u32[]{:S(2)}, u32[]{:S(2)}) %collective-permute-start.7) | collective-permute-done | bytes 262176 | tf_op jit(solution)/shard_map/ppermute | solution.py:201
  66.1 3.6 %collective-permute-done.6 = bf16[128,1024]{1,0:T(8,128)(2,1)S(1)} collective-permute-done((bf16[128,1024]{1,0:T(8,128)(2,1)S(1)}, bf16[128,1024]{1,0:T(8,128)(2,1)S(1)}, u32[]{:S(2)}, u32[]{:S(2)}) %collective-permute-start.6) | collective-permute-done | bytes 262176 | tf_op jit(solution)/shard_map/ppermute | solution.py:201
  69.7 0.2 collective-permute-done.5
  69.9 0.1 pad_maximum_fusion.2
  70.0 0.1 constant_dynamic-slice_fusion.11
  70.1 0.1 pad_maximum_fusion.3.enter_ref
  70.3 9.5 %gate.1 = (f32[512,4096]{1,0:T(8,128)}, f32[512,128]{1,0:T(8,128)S(1)}) custom-call(f32[512,4096]{1,0:T(8,128)} %intra.1.y_ref, bf16[512,4096]{1,0:T(8,128)(2,1)} %z_ref.1, bf16[512,512]{1,0:T(8,128)(2,1)S(1)} %get-tuple-element.17.c_ref, bf16[512,128]{1,0:T(8,128)(2,1)S(1)} %pad_maximum_fusion.6.link_ref, bf16[4,128,1024]{2,1,0:T(8,128)(2,1)S(1)} %pad_maximum_fusion.3.enter_ref), custom_call_target="tpu_custom_call" | custom-call | tf_op jit(solution)/shard_map/gate/pallas_call | solution.py:356
  79.8 0.1 reduce_sum.9
  79.9 0.1 copy.58
  80.2 1.5 %collective-permute-done.8 = f32[512,1]{1,0:T(8,128)S(1)} collective-permute-done((f32[512,1]{1,0:T(8,128)S(1)}, f32[512,1]{1,0:T(8,128)S(1)}, u32[]{:S(2)}, u32[]{:S(2)}) %collective-permute-start.8) | collective-permute-done | bytes 2080 | tf_op jit(solution)/shard_map/ppermute | solution.py:376
  81.7 6.1 %norm.1 = bf16[512,4096]{1,0:T(8,128)(2,1)} custom-call(f32[512,4096]{1,0:T(8,128)} %get-tuple-element.21.gated_ref, f32[512,1]{1,0:T(8,128)S(1)} %add.152.total_ref, f32[1,4096]{1,0:T(1,128)S(1)} %bitcast.133), custom_call_target="tpu_custom_call" | custom-call | tf_op jit(solution)/shard_map/norm/pallas_call | solution.py:378
  (43 shorter events, 0.8 us)
Async XLA Ops:
  0.0 10.8 %copy-start.4 = (s32[512]{0:T(512)S(1)}, s32[512]{0:T(512)}, u32[]{:S(2)}) copy-start(s32[512]{0:T(512)} %param.25) | copy-start | bytes 6148
  0.0 10.5 %copy-start.6 = (f32[2,512]{1,0:T(2,128)S(1)}, f32[2,512]{1,0:T(2,128)}, u32[]{:S(2)}) copy-start(f32[2,512]{1,0:T(2,128)} %param.20) | copy-start | bytes 12292
  0.0 10.5 %copy-start.5 = (bf16[4,2,512]{2,1,0:T(2,128)(2,1)S(1)}, bf16[4,2,512]{2,1,0:T(2,128)(2,1)}, u32[]{:S(2)}) copy-start(bf16[4,2,512]{2,1,0:T(2,128)(2,1)} %param.18) | copy-start | bytes 24580
  0.0 10.5 %copy-start.7 = (f32[64]{0:T(128)S(1)}, f32[64]{0:T(128)}, u32[]{:S(2)}) copy-start(f32[64]{0:T(128)} %param.23) | copy-start | bytes 772
  2.5 11.2 %collective-permute-start = (bf16[8,5248]{1,0:T(8,128)(2,1)S(1)}, bf16[8,5248]{1,0:T(8,128)(2,1)S(1)}, u32[]{:S(2)}, u32[]{:S(2)}) collective-permute-start(bf16[8,5248]{1,0:T(8,128)(2,1)S(1)} %pad_maximum_fusion.7), channel_id=1, source_target_pairs={{0,2},{2,4},{4,6},{6,8},{8,10},{10,12},{12,14},{14,16},{16,18},{18... | collective-permute-start | bytes 251912 | tf_op jit(solution)/shard_map/ppermute | solution.py:248
  9.8 2.5 %copy-start.3 = (bf16[512,2,512]{2,1,0:T(2,128)(2,1)S(1)}, bf16[512,2,512]{2,1,0:T(2,128)(2,1)}, u32[]{:S(2)}) copy-start(bf16[512,2,512]{2,1,0:T(2,128)(2,1)} %param.14) | copy-start | bytes 3145732
  15.1 0.8 copy-start
  15.1 0.8 copy-start.1
  29.9 14.9 %collective-permute-start.3 = (bf16[144,1024]{1,0:T(8,128)(2,1)S(1)}, bf16[144,1024]{1,0:T(8,128)(2,1)S(1)}, u32[]{:S(2)}, u32[]{:S(2)}) collective-permute-start(bf16[144,1024]{1,0:T(8,128)(2,1)S(1)} %get-tuple-element.43), channel_id=1, source_target_pairs={{0,6},{2,4},{4,2},{6,0},{8,14},{10,12},{12,10},{14,8},{16,22},{18,... | collective-permute-start | bytes 884744 | tf_op jit(solution)/shard_map/ppermute | solution.py:201
  32.4 13.2 %collective-permute-start.2 = (bf16[144,1024]{1,0:T(8,128)(2,1)S(1)}, bf16[144,1024]{1,0:T(8,128)(2,1)S(1)}, u32[]{:S(2)}, u32[]{:S(2)}) collective-permute-start(bf16[144,1024]{1,0:T(8,128)(2,1)S(1)} %get-tuple-element.44), channel_id=1, source_target_pairs={{0,4},{2,6},{4,0},{6,2},{8,12},{10,14},{12,8},{14,10},{16,20},{18,... | collective-permute-start | bytes 884744 | tf_op jit(solution)/shard_map/ppermute | solution.py:201
  32.9 12.8 %collective-permute-start.1 = (bf16[144,1024]{1,0:T(8,128)(2,1)S(1)}, bf16[144,1024]{1,0:T(8,128)(2,1)S(1)}, u32[]{:S(2)}, u32[]{:S(2)}) collective-permute-start(bf16[144,1024]{1,0:T(8,128)(2,1)S(1)} %get-tuple-element.45), channel_id=1, source_target_pairs={{0,2},{2,0},{4,6},{6,4},{8,10},{10,8},{12,14},{14,12},{16,18},{18,... | collective-permute-start | bytes 884744 | tf_op jit(solution)/shard_map/ppermute | solution.py:201
  46.2 9.1 %collective-permute-start.4 = (bf16[128,1024]{1,0:T(8,128)(2,1)S(1)}, bf16[128,1024]{1,0:T(8,128)(2,1)S(1)}, u32[]{:S(2)}, u32[]{:S(2)}) collective-permute-start(bf16[128,1024]{1,0:T(8,128)(2,1)S(1)} %fusion.6), channel_id=1, source_target_pairs={{0,8},{2,10},{4,12},{6,14},{8,16},{10,18},{12,20},{14,22},{16,24},... | collective-permute-start | bytes 786440 | tf_op jit(solution)/shard_map/ppermute | solution.py:216
  55.8 10.2 %collective-permute-start.7 = (bf16[128,1024]{1,0:T(8,128)(2,1)S(1)}, bf16[128,1024]{1,0:T(8,128)(2,1)S(1)}, u32[]{:S(2)}, u32[]{:S(2)}) collective-permute-start(bf16[128,1024]{1,0:T(8,128)(2,1)S(1)} %get-tuple-element.51), channel_id=1, source_target_pairs={{0,6},{2,4},{4,2},{6,0},{8,14},{10,12},{12,10},{14,8},{16,22},{18,... | collective-permute-start | bytes 786440 | tf_op jit(solution)/shard_map/ppermute | solution.py:201
  56.9 12.8 %collective-permute-start.6 = (bf16[128,1024]{1,0:T(8,128)(2,1)S(1)}, bf16[128,1024]{1,0:T(8,128)(2,1)S(1)}, u32[]{:S(2)}, u32[]{:S(2)}) collective-permute-start(bf16[128,1024]{1,0:T(8,128)(2,1)S(1)} %get-tuple-element.52), channel_id=1, source_target_pairs={{0,4},{2,6},{4,0},{6,2},{8,12},{10,14},{12,8},{14,10},{16,20},{18,... | collective-permute-start | bytes 786440 | tf_op jit(solution)/shard_map/ppermute | solution.py:201
  58.9 11.0 %collective-permute-start.5 = (bf16[128,1024]{1,0:T(8,128)(2,1)S(1)}, bf16[128,1024]{1,0:T(8,128)(2,1)S(1)}, u32[]{:S(2)}, u32[]{:S(2)}) collective-permute-start(bf16[128,1024]{1,0:T(8,128)(2,1)S(1)} %get-tuple-element.53), channel_id=1, source_target_pairs={{0,2},{2,0},{4,6},{6,4},{8,10},{10,8},{12,14},{14,12},{16,18},{18,... | collective-permute-start | bytes 786440 | tf_op jit(solution)/shard_map/ppermute | solution.py:201
  79.8 1.9 %copy-start.2 = (f32[4096]{0:T(1024)S(1)}, f32[4096]{0:T(1024)}, u32[]{:S(2)}) copy-start(f32[4096]{0:T(1024)} %param.24) | copy-start | bytes 49156
  80.1 1.6 %collective-permute-start.8 = (f32[512,1]{1,0:T(8,128)S(1)}, f32[512,1]{1,0:T(8,128)S(1)}, u32[]{:S(2)}, u32[]{:S(2)}) collective-permute-start(f32[512,1]{1,0:T(8,128)S(1)} %copy.58), channel_id=1, source_target_pairs={{0,1},{1,0},{2,3},{3,2},{4,5},{5,4},{6,7},{7,6},{8,9},{9,8},{10,11... | collective-permute-start | bytes 6152 | tf_op jit(solution)/shard_map/ppermute | solution.py:376

commit v5 on v4

--- a/solution.py
+++ b/solution.py
@@ -374,10 +374,10 @@
     own = total
     for k in range(1, count):
         total = total + lax.ppermute(own, "tp", [(i, (i + k) % count) for i in range(count)])
-    part = rows // 4
+    part = rows // 2
     return pl.pallas_call(
         functools.partial(norm_kernel, channels=inner * count),
-        grid=(4,),
+        grid=(2,),
         in_specs=[
             pl.BlockSpec((part, inner), lambda r: (r, 0)),
             full(rows, 1),

time: 88.4 us -> 87.6 us (level)
  Pallas kernels: 39.6 us -> 38.7 us
  transfers between devices with their start and end apart: 9 -> 9, of which waited for: 7 -> 7; matrix products, arithmetic and copies ran while one was open for 7% -> 8% of each run, Pallas kernels for 13% -> 13%
where the time goes in v5:
time: 87.6 us; the launch traced here: 87 us
  Pallas kernels  38.7 us (44%)
  waiting for transfers between devices  18.3 us (21%)
  starting transfers between devices  15.5 us (18%)
  local copies, waits for them, and re-layouts  8.78 us (10%)
  other arithmetic  4.83 us (6%)
    pallas_call x1, Pallas kernels, on_device(): pl.pallas_call(local_kernel, grid=(groups,), in_specs=[wide(rows), wide(R...  12.7 us
    ppermute x6, waiting for transfers between devices, swap(): lax.ppermute(pick(array, place ^ k), axis, [(i, i ^ k) for i in range(cou...  11.3 us
    pallas_call x1, Pallas kernels, on_device(): pl.pallas_call(intra_kernel, grid=(groups,), in_specs=[wide(rows), state_...  11.2 us
    pallas_call x1, Pallas kernels, on_device(): pl.pallas_call(gate_kernel, grid=(groups,), in_specs=[wide(rows), wide(ro...  9.51 us
    ppermute x6, starting transfers between devices, swap(): lax.ppermute(pick(array, place ^ k), axis, [(i, i ^ k) for i in range(cou...  7.11 us
    ppermute x1, waiting for transfers between devices, exchange(): lax.ppermute(run.astype(BF16), axis, [(i, i + plane) for i in range(count...  5.49 us
    pallas_call x1, Pallas kernels, on_device(): pl.pallas_call(functools.partial(norm_kernel, channels=inner * count), gr...  5.25 us
    ppermute x1, starting transfers between devices, on_device(): rim = lax.ppermute(jnp.concatenate(ends, axis=1), 'seq', route)  4.84 us
  transfers between devices with their start and end apart: 9, of which 7 were waited for; matrix products, arithmetic and copies ran while one was open for 8% of the time, Pallas kernels for 13%

profile of v5, /device:TPU:0, one launch (start us, length us, event | category | flops | bytes accessed | tf_op | source)
XLA Modules:
  0.0 87.0 jit_solution(13399871257910764441)
XLA Ops:
  0.0 0.8 convert.12
  0.8 0.1 slice.95
  0.8 0.7 slice_bitcast_fusion
  1.6 0.8 slice.93
  2.5 4.8 %collective-permute-start = (bf16[8,5248]{1,0:T(8,128)(2,1)S(1)}, bf16[8,5248]{1,0:T(8,128)(2,1)S(1)}, u32[]{:S(2)}, u32[]{:S(2)}) collective-permute-start(bf16[8,5248]{1,0:T(8,128)(2,1)S(1)} %pad_maximum_fusion.7), channel_id=1, source_target_pairs={{0,2},{2,4},{4,6},{6,8},{8,10},{10,12},{12,14},{14,16},{16,18},{18... | collective-permute-start | bytes 251912 | tf_op jit(solution)/shard_map/ppermute | solution.py:248
  7.4 0.7 reshape.331.idr_ref
  8.1 0.7 negate_multiply_fusion
  8.7 1.1 %broadcast_multiply_fusion.1 = (f32[512,64]{0,1:T(8,128)S(1)}, f32[512,64]{0,1:T(8,128)S(1)}) fusion(f32[64]{0:T(128)S(1)} %negate_multiply_fusion, f32[512,64]{0,1:T(8,128)} %param.16, f32[64]{0:T(128)} %param.21), kind=kLoop, calls=%fused_computation.63 | loop fusion | flops 262144 | bytes 393728 | tf_op jit(solution)/shard_map/mul | solution.py:259
  9.8 0.4 convolution_bitcast_fusion
  10.2 0.2 slice_reduce_fusion
  10.4 0.1 copy.50
  10.6 0.1 reshape_reshape.3.skip_ref
  10.7 0.1 reshape.334
  10.8 0.1 copy.55.ids_ref
  11.0 1.3 %copy.51 = f32[512,4,16]{2,0,1:T(8,128)} copy(f32[512,4,16]{0,2,1:T(8,128)S(1)} %reshape.334) | data formatting | bytes 262144 | tf_op jit(solution)/shard_map/reshape | solution.py:270
  12.3 1.2 %copy.62 = bf16[64,8,2,512]{3,1,2,0:T(8,128)(2,1)} copy(bf16[64,8,2,512]{3,2,1,0:T(2,128)(2,1)S(1)} %bitcast.136) | data formatting | bytes 2097152
  13.5 0.2 slice_reduce_fusion.1
  13.7 0.1 convert_reduce_fusion
  13.8 0.1 pad_add_fusion
  13.9 0.1 slice.103
  14.0 0.1 slice_compare_fusion.2
  14.2 0.1 copy.49.counted_ref
  14.4 0.1 mul.158
  14.5 0.1 broadcast_in_dim.38
  14.6 0.1 mul.159
  14.7 0.1 broadcast_in_dim.39
  14.8 0.1 reshape.333.row_gain_ref
  14.9 0.1 broadcast_multiply_fusion
  15.1 0.1 copy.54
  15.3 0.1 copy.48
  15.5 0.1 pad_maximum_fusion.4.tail_ref
  15.6 0.2 copy-done
  15.8 12.7 %local.1 = (bf16[512,4096]{1,0:T(8,128)(2,1)}, bf16[512,512]{1,0:T(8,128)(2,1)S(1)}, bf16[512,512]{1,0:T(8,128)(2,1)S(1)}, f32[4,128,1024]{2,1,0:T(8,128)}, bf16[4,144,1024]{2,1,0:T(8,128)(2,1)}) custom-call(bf16[512,4096]{1,0:T(8,128)(2,1)} %x_ref.1, bf16[8,5248]{1,0:T(8,128)(2,1)S(1)} %collective-permute-done.rim_ref.rimb_ref.rimc_ref, ...), custom_call_target="tpu_custom_call" | custom-call | flops 1073741824 | bytes 31457280 | tf_op jit(solution)/shard_map/local/pallas_call | solution.py:295
  28.6 1.3 %constant_dynamic-slice_fusion.13 = (bf16[1,144,1024]{2,1,0:T(8,128)(2,1)S(1)}, bf16[144,1024]{1,0:T(8,128)(2,1)S(1)}, bf16[144,1024]{1,0:T(8,128)(2,1)S(1)}, bf16[144,1024]{1,0:T(8,128)(2,1)S(1)}) fusion(bf16[4,144,1024]{2,1,0:T(8,128)(2,1)} %get-tuple-element.14, s32[]{:T(128)S(6)} %select_n.44, s32[]{:T(128)S(6)} %select_n.47, s32[]{:T(128)S(6)} %select_n.46, ...), kind=kLoop, calls=%fused_computation.81 | loop fusion | bytes 2359312 | tf_op jit(solution)/shard_map/jit(dynamic_index_in_dim)/dynamic_slice | solution.py:195
  29.9 2.5 %collective-permute-start.3 = (bf16[144,1024]{1,0:T(8,128)(2,1)S(1)}, bf16[144,1024]{1,0:T(8,128)(2,1)S(1)}, u32[]{:S(2)}, u32[]{:S(2)}) collective-permute-start(bf16[144,1024]{1,0:T(8,128)(2,1)S(1)} %get-tuple-element.43), channel_id=1, source_target_pairs={{0,6},{2,4},{4,2},{6,0},{8,14},{10,12},{12,10},{14,8},{16,22},{18,... | collective-permute-start | bytes 884744 | tf_op jit(solution)/shard_map/ppermute | solution.py:201
  32.4 0.5 collective-permute-start.2
  32.9 0.5 collective-permute-start.1
  33.4 0.1 pad_maximum_fusion.5.link_ref
  33.6 11.2 %intra.1.y_ref = f32[512,4096]{1,0:T(8,128)} custom-call(bf16[512,4096]{1,0:T(8,128)(2,1)} %get-tuple-element.15.x_ref, bf16[512,512]{1,0:T(8,128)(2,1)S(1)} %get-tuple-element.16.b_ref, bf16[512,512]{1,0:T(8,128)(2,1)S(1)} %get-tuple-element.17.c_ref, f32[4,512,16]{2,1,0:T(8,128)} %bitcast.137, f32[4,2,16,256]{3,2,1,0:T(8,128)S(1)} %bitcast.127, ...), custom_call_target="tpu_custom_call" | custom-call | flops 21474836480 | bytes 104857600 | tf_op jit(solution)/shard_map/intra/pallas_call | solution.py:332
  44.8 0.9 %collective-permute-done.2 = bf16[144,1024]{1,0:T(8,128)(2,1)S(1)} collective-permute-done((bf16[144,1024]{1,0:T(8,128)(2,1)S(1)}, bf16[144,1024]{1,0:T(8,128)(2,1)S(1)}, u32[]{:S(2)}, u32[]{:S(2)}) %collective-permute-start.2) | collective-permute-done | bytes 294944 | tf_op jit(solution)/shard_map/ppermute | solution.py:201
  45.6 0.1 collective-permute-done.1
  45.7 0.1 pad_maximum_fusion
  46.0 0.2 fusion.6
  46.2 3.5 %collective-permute-start.4 = (bf16[128,1024]{1,0:T(8,128)(2,1)S(1)}, bf16[128,1024]{1,0:T(8,128)(2,1)S(1)}, u32[]{:S(2)}, u32[]{:S(2)}) collective-permute-start(bf16[128,1024]{1,0:T(8,128)(2,1)S(1)} %fusion.6), channel_id=1, source_target_pairs={{0,8},{2,10},{4,12},{6,14},{8,16},{10,18},{12,20},{14,22},{16,24},... | collective-permute-start | bytes 786440 | tf_op jit(solution)/shard_map/ppermute | solution.py:216
  49.7 0.1 copy.56
  49.8 5.5 %collective-permute-done.4 = bf16[128,1024]{1,0:T(8,128)(2,1)S(1)} collective-permute-done((bf16[128,1024]{1,0:T(8,128)(2,1)S(1)}, bf16[128,1024]{1,0:T(8,128)(2,1)S(1)}, u32[]{:S(2)}, u32[]{:S(2)}) %collective-permute-start.4) | collective-permute-done | bytes 262176 | tf_op jit(solution)/shard_map/ppermute | solution.py:216
  55.3 0.3 fusion.9
  55.6 0.1 pad_maximum_fusion.1
  55.8 0.1 constant_dynamic-slice_fusion.12
  55.8 1.0 %collective-permute-start.7 = (bf16[128,1024]{1,0:T(8,128)(2,1)S(1)}, bf16[128,1024]{1,0:T(8,128)(2,1)S(1)}, u32[]{:S(2)}, u32[]{:S(2)}) collective-permute-start(bf16[128,1024]{1,0:T(8,128)(2,1)S(1)} %get-tuple-element.51), channel_id=1, source_target_pairs={{0,6},{2,4},{4,2},{6,0},{8,14},{10,12},{12,10},{14,8},{16,22},{18,... | collective-permute-start | bytes 786440 | tf_op jit(solution)/shard_map/ppermute | solution.py:201
  56.9 2.0 %collective-permute-start.6 = (bf16[128,1024]{1,0:T(8,128)(2,1)S(1)}, bf16[128,1024]{1,0:T(8,128)(2,1)S(1)}, u32[]{:S(2)}, u32[]{:S(2)}) collective-permute-start(bf16[128,1024]{1,0:T(8,128)(2,1)S(1)} %get-tuple-element.52), channel_id=1, source_target_pairs={{0,4},{2,6},{4,0},{6,2},{8,12},{10,14},{12,8},{14,10},{16,20},{18,... | collective-permute-start | bytes 786440 | tf_op jit(solution)/shard_map/ppermute | solution.py:201
  58.9 0.5 collective-permute-start.5
  59.4 0.1 pad_maximum_fusion.6.link_ref
  59.6 6.5 %collective-permute-done.7 = bf16[128,1024]{1,0:T(8,128)(2,1)S(1)} collective-permute-done((bf16[128,1024]{1,0:T(8,128)(2,1)S(1)}, bf16[128,1024]{1,0:T(8,128)(2,1)S(1)}, u32[]{:S(2)}, u32[]{:S(2)}) %collective-permute-start.7) | collective-permute-done | bytes 262176 | tf_op jit(solution)/shard_map/ppermute | solution.py:201
  66.1 3.6 %collective-permute-done.6 = bf16[128,1024]{1,0:T(8,128)(2,1)S(1)} collective-permute-done((bf16[128,1024]{1,0:T(8,128)(2,1)S(1)}, bf16[128,1024]{1,0:T(8,128)(2,1)S(1)}, u32[]{:S(2)}, u32[]{:S(2)}) %collective-permute-start.6) | collective-permute-done | bytes 262176 | tf_op jit(solution)/shard_map/ppermute | solution.py:201
  69.7 0.2 collective-permute-done.5
  69.9 0.1 pad_maximum_fusion.2
  70.0 0.1 constant_dynamic-slice_fusion.11
  70.1 0.1 pad_maximum_fusion.3.enter_ref
  70.3 9.5 %gate.1 = (f32[512,4096]{1,0:T(8,128)}, f32[512,128]{1,0:T(8,128)S(1)}) custom-call(f32[512,4096]{1,0:T(8,128)} %intra.1.y_ref, bf16[512,4096]{1,0:T(8,128)(2,1)} %z_ref.1, bf16[512,512]{1,0:T(8,128)(2,1)S(1)} %get-tuple-element.17.c_ref, bf16[512,128]{1,0:T(8,128)(2,1)S(1)} %pad_maximum_fusion.6.link_ref, bf16[4,128,1024]{2,1,0:T(8,128)(2,1)S(1)} %pad_maximum_fusion.3.enter_ref), custom_call_target="tpu_custom_call" | custom-call | tf_op jit(solution)/shard_map/gate/pallas_call | solution.py:356
  79.8 0.1 reduce_sum.9
  79.9 0.1 copy.58
  80.2 1.5 %collective-permute-done.8 = f32[512,1]{1,0:T(8,128)S(1)} collective-permute-done((f32[512,1]{1,0:T(8,128)S(1)}, f32[512,1]{1,0:T(8,128)S(1)}, u32[]{:S(2)}, u32[]{:S(2)}) %collective-permute-start.8) | collective-permute-done | bytes 2080 | tf_op jit(solution)/shard_map/ppermute | solution.py:376
  81.7 5.3 %norm.1 = bf16[512,4096]{1,0:T(8,128)(2,1)} custom-call(f32[512,4096]{1,0:T(8,128)} %get-tuple-element.21.gated_ref, f32[512,1]{1,0:T(8,128)S(1)} %add.152.total_ref, f32[1,4096]{1,0:T(1,128)S(1)} %bitcast.133), custom_call_target="tpu_custom_call" | custom-call | tf_op jit(solution)/shard_map/norm/pallas_call | solution.py:378
  (43 shorter events, 0.8 us)
Async XLA Ops:
  0.0 10.8 %copy-start.4 = (s32[512]{0:T(512)S(1)}, s32[512]{0:T(512)}, u32[]{:S(2)}) copy-start(s32[512]{0:T(512)} %param.25) | copy-start | bytes 6148
  0.0 10.5 %copy-start.6 = (f32[2,512]{1,0:T(2,128)S(1)}, f32[2,512]{1,0:T(2,128)}, u32[]{:S(2)}) copy-start(f32[2,512]{1,0:T(2,128)} %param.20) | copy-start | bytes 12292
  0.0 10.5 %copy-start.5 = (bf16[4,2,512]{2,1,0:T(2,128)(2,1)S(1)}, bf16[4,2,512]{2,1,0:T(2,128)(2,1)}, u32[]{:S(2)}) copy-start(bf16[4,2,512]{2,1,0:T(2,128)(2,1)} %param.18) | copy-start | bytes 24580
  0.0 10.5 %copy-start.7 = (f32[64]{0:T(128)S(1)}, f32[64]{0:T(128)}, u32[]{:S(2)}) copy-start(f32[64]{0:T(128)} %param.23) | copy-start | bytes 772
  2.5 11.2 %collective-permute-start = (bf16[8,5248]{1,0:T(8,128)(2,1)S(1)}, bf16[8,5248]{1,0:T(8,128)(2,1)S(1)}, u32[]{:S(2)}, u32[]{:S(2)}) collective-permute-start(bf16[8,5248]{1,0:T(8,128)(2,1)S(1)} %pad_maximum_fusion.7), channel_id=1, source_target_pairs={{0,2},{2,4},{4,6},{6,8},{8,10},{10,12},{12,14},{14,16},{16,18},{18... | collective-permute-start | bytes 251912 | tf_op jit(solution)/shard_map/ppermute | solution.py:248
  9.8 2.5 %copy-start.3 = (bf16[512,2,512]{2,1,0:T(2,128)(2,1)S(1)}, bf16[512,2,512]{2,1,0:T(2,128)(2,1)}, u32[]{:S(2)}) copy-start(bf16[512,2,512]{2,1,0:T(2,128)(2,1)} %param.14) | copy-start | bytes 3145732
  15.1 0.8 copy-start
  15.1 0.8 copy-start.1
  29.9 14.9 %collective-permute-start.3 = (bf16[144,1024]{1,0:T(8,128)(2,1)S(1)}, bf16[144,1024]{1,0:T(8,128)(2,1)S(1)}, u32[]{:S(2)}, u32[]{:S(2)}) collective-permute-start(bf16[144,1024]{1,0:T(8,128)(2,1)S(1)} %get-tuple-element.43), channel_id=1, source_target_pairs={{0,6},{2,4},{4,2},{6,0},{8,14},{10,12},{12,10},{14,8},{16,22},{18,... | collective-permute-start | bytes 884744 | tf_op jit(solution)/shard_map/ppermute | solution.py:201
  32.4 13.2 %collective-permute-start.2 = (bf16[144,1024]{1,0:T(8,128)(2,1)S(1)}, bf16[144,1024]{1,0:T(8,128)(2,1)S(1)}, u32[]{:S(2)}, u32[]{:S(2)}) collective-permute-start(bf16[144,1024]{1,0:T(8,128)(2,1)S(1)} %get-tuple-element.44), channel_id=1, source_target_pairs={{0,4},{2,6},{4,0},{6,2},{8,12},{10,14},{12,8},{14,10},{16,20},{18,... | collective-permute-start | bytes 884744 | tf_op jit(solution)/shard_map/ppermute | solution.py:201
  32.9 12.8 %collective-permute-start.1 = (bf16[144,1024]{1,0:T(8,128)(2,1)S(1)}, bf16[144,1024]{1,0:T(8,128)(2,1)S(1)}, u32[]{:S(2)}, u32[]{:S(2)}) collective-permute-start(bf16[144,1024]{1,0:T(8,128)(2,1)S(1)} %get-tuple-element.45), channel_id=1, source_target_pairs={{0,2},{2,0},{4,6},{6,4},{8,10},{10,8},{12,14},{14,12},{16,18},{18,... | collective-permute-start | bytes 884744 | tf_op jit(solution)/shard_map/ppermute | solution.py:201
  46.2 9.1 %collective-permute-start.4 = (bf16[128,1024]{1,0:T(8,128)(2,1)S(1)}, bf16[128,1024]{1,0:T(8,128)(2,1)S(1)}, u32[]{:S(2)}, u32[]{:S(2)}) collective-permute-start(bf16[128,1024]{1,0:T(8,128)(2,1)S(1)} %fusion.6), channel_id=1, source_target_pairs={{0,8},{2,10},{4,12},{6,14},{8,16},{10,18},{12,20},{14,22},{16,24},... | collective-permute-start | bytes 786440 | tf_op jit(solution)/shard_map/ppermute | solution.py:216
  55.8 10.2 %collective-permute-start.7 = (bf16[128,1024]{1,0:T(8,128)(2,1)S(1)}, bf16[128,1024]{1,0:T(8,128)(2,1)S(1)}, u32[]{:S(2)}, u32[]{:S(2)}) collective-permute-start(bf16[128,1024]{1,0:T(8,128)(2,1)S(1)} %get-tuple-element.51), channel_id=1, source_target_pairs={{0,6},{2,4},{4,2},{6,0},{8,14},{10,12},{12,10},{14,8},{16,22},{18,... | collective-permute-start | bytes 786440 | tf_op jit(solution)/shard_map/ppermute | solution.py:201
  56.9 12.8 %collective-permute-start.6 = (bf16[128,1024]{1,0:T(8,128)(2,1)S(1)}, bf16[128,1024]{1,0:T(8,128)(2,1)S(1)}, u32[]{:S(2)}, u32[]{:S(2)}) collective-permute-start(bf16[128,1024]{1,0:T(8,128)(2,1)S(1)} %get-tuple-element.52), channel_id=1, source_target_pairs={{0,4},{2,6},{4,0},{6,2},{8,12},{10,14},{12,8},{14,10},{16,20},{18,... | collective-permute-start | bytes 786440 | tf_op jit(solution)/shard_map/ppermute | solution.py:201
  58.9 11.0 %collective-permute-start.5 = (bf16[128,1024]{1,0:T(8,128)(2,1)S(1)}, bf16[128,1024]{1,0:T(8,128)(2,1)S(1)}, u32[]{:S(2)}, u32[]{:S(2)}) collective-permute-start(bf16[128,1024]{1,0:T(8,128)(2,1)S(1)} %get-tuple-element.53), channel_id=1, source_target_pairs={{0,2},{2,0},{4,6},{6,4},{8,10},{10,8},{12,14},{14,12},{16,18},{18,... | collective-permute-start | bytes 786440 | tf_op jit(solution)/shard_map/ppermute | solution.py:201
  79.8 1.9 %copy-start.2 = (f32[4096]{0:T(1024)S(1)}, f32[4096]{0:T(1024)}, u32[]{:S(2)}) copy-start(f32[4096]{0:T(1024)} %param.24) | copy-start | bytes 49156
  80.1 1.6 %collective-permute-start.8 = (f32[512,1]{1,0:T(8,128)S(1)}, f32[512,1]{1,0:T(8,128)S(1)}, u32[]{:S(2)}, u32[]{:S(2)}) collective-permute-start(f32[512,1]{1,0:T(8,128)S(1)} %copy.58), channel_id=1, source_target_pairs={{0,1},{1,0},{2,3},{3,2},{4,5},{5,4},{6,7},{7,6},{8,9},{9,8},{10,11... | collective-permute-start | bytes 6152 | tf_op jit(solution)/shard_map/ppermute | solution.py:376
